TPU v7x, 256 devices: a whole 4x4x8 slice. The times are simulated.
256 devices in a mesh: fsdp: 64 (over z, x, core), tp: 4 (over y).
Axes of the slice: x: 4, y: 4, z: 8, core: 2. Of those that a mesh axis runs over, the one named last changes fastest.
Arguments:
- tokens: bfloat16 [4096, 3072], P('fsdp', 'tp'), may hold values from -6 to 6
- cotangent: bfloat16 [4096, 3072], P('fsdp', 'tp'), may hold values from -0.52734375 to 0.52734375
- expert_ids: int32 [4096, 2], P('fsdp'), may hold values from 0 to 3, all different within a row; in each aligned block of 64 rows (0 to 63, 64 to 127, ...) at most 36 rows name the same one
- route_weights: float32 [4096, 2], P('fsdp'), may hold values from 0.2 to 1
- gate_weight: bfloat16 [3072, 32768], P('tp', 'fsdp'), may hold values from -0.109375 to 0.109375
- up_weight: bfloat16 [3072, 32768], P('tp', 'fsdp'), may hold values from -0.109375 to 0.109375
- down_weight: bfloat16 [32768, 3072], P('fsdp', 'tp'), may hold values from -0.0625 to 0.0625
- projector: bfloat16 [4, 3072, 512], P(None, 'tp'), may hold values from -0.109375 to 0.109375
- first_moment: float32 [32768, 512], P('fsdp'), may hold values from -3 to 3
- second_moment: float32 [32768, 512], P('fsdp'), may hold values from 0.05 to 1
Outputs:
- mixed: bfloat16 [4096, 3072], P('fsdp', 'tp')
- down_update: float32 [32768, 3072], P('fsdp', 'tp')
- new_first: float32 [32768, 512], P('fsdp')
- new_second: float32 [32768, 512], P('fsdp')
Inputs may be any that keep to these rules, and one draw needn't show every extreme that they name: `expert_ids`: the two ids of a token differ. In each aligned block of 64 tokens (the tokens of one index of fsdp) no expert is named by more than 36 tokens, a bound that some block reaches.
All inputs are finite; a program needn't handle non-finite values.
Results may differ from a plain program's by a relative error of at most 0.022.
Values may be sent and summed in bfloat16 or wider, within the bound.
A program may use at most 128 MiB of HBM per device.

v0:
```python
import jax
import jax.numpy as jnp
from jax import lax
from jax.sharding import PartitionSpec as P

EXPERTS = 4
MOST = 36


def body(
    tokens,
    cotangent,
    expert_ids,
    route_weights,
    gate_weight,
    up_weight,
    down_weight,
    projector,
    first_moment,
    second_moment,
):
    groups = lax.axis_size("fsdp") // EXPERTS
    sources = lax.axis_size("fsdp")
    features = tokens.shape[1]
    slot_total = EXPERTS * MOST
    onehot = (expert_ids[:, :, None] == jnp.arange(EXPERTS, dtype=jnp.int32)[None, None, :]).astype(
        jnp.int32
    )
    per_token = jnp.sum(onehot, axis=1)
    before = jnp.cumsum(per_token, axis=0) - per_token
    position = jnp.sum(onehot * before[:, None, :], axis=2)
    slot_id = expert_ids * MOST + position
    matches = jnp.arange(slot_total, dtype=jnp.int32)[:, None, None] == slot_id[None, :, :]
    picker = jnp.any(matches, axis=2).astype(jnp.bfloat16)
    slot_weight = jnp.sum(jnp.where(matches, route_weights[None, :, :], 0.0), axis=(1, 2))
    local_rows = jnp.dot(picker, tokens, preferred_element_type=jnp.float32).astype(jnp.bfloat16)
    local_grads = (
        jnp.dot(picker, cotangent, preferred_element_type=jnp.float32) * slot_weight[:, None]
    ).astype(jnp.bfloat16)
    send_rows = jnp.repeat(local_rows.reshape(EXPERTS, MOST, features), groups, axis=0)
    send_grads = jnp.repeat(local_grads.reshape(EXPERTS, MOST, features), groups, axis=0)
    got_rows, got_grads = (
        lax.all_to_all(send_rows, "fsdp", split_axis=0, concat_axis=0, tiled=True),
        lax.all_to_all(send_grads, "fsdp", split_axis=0, concat_axis=0, tiled=True),
    )
    routed_grads = got_grads.reshape(sources * MOST, features)
    routed_rows = got_rows.reshape(sources * MOST, features)
    gate_cols, up_cols = (
        lax.all_to_all(gate_weight, "tp", split_axis=1, concat_axis=0, tiled=True),
        lax.all_to_all(up_weight, "tp", split_axis=1, concat_axis=0, tiled=True),
    )
    piece = lax.all_gather(routed_rows, "tp", axis=1, tiled=True)
    gate_part = jnp.dot(piece, gate_cols, preferred_element_type=jnp.float32)
    up_part = jnp.dot(piece, up_cols, preferred_element_type=jnp.float32)
    hidden_part = (jax.nn.silu(gate_part) * up_part).astype(jnp.bfloat16)
    hidden = lax.all_gather(hidden_part, "tp", axis=1, tiled=True)
    partial_out = jnp.dot(hidden, down_weight, preferred_element_type=jnp.float32)
    grad_block = lax.dot_general(
        hidden, routed_grads, (((0,), (0,)), ((), ())), preferred_element_type=jnp.float32
    )
    returned = lax.all_to_all(
        partial_out.reshape(sources, MOST, features).astype(jnp.bfloat16),
        "fsdp",
        split_axis=0,
        concat_axis=0,
        tiled=True,
    ).astype(jnp.float32)
    summed = jnp.sum(returned.reshape(EXPERTS, groups, MOST, features), axis=1)
    mixed = route_weights[:, 0:1] * summed[expert_ids[:, 0], position[:, 0]]
    mixed = mixed + route_weights[:, 1:2] * summed[expert_ids[:, 1], position[:, 1]]
    own_expert = lax.axis_index("fsdp") // groups
    basis = lax.dynamic_index_in_dim(projector, own_expert, 0, keepdims=False).astype(jnp.float32)
    low_part = jnp.dot(grad_block, basis, precision=lax.Precision.HIGHEST)
    low = lax.psum(low_part.astype(jnp.bfloat16), "tp").astype(jnp.float32)
    new_first = 0.9 * first_moment + 0.1 * low
    new_second = 0.999 * second_moment + 0.001 * low * low
    bias_one = 1.0 - 0.9**10
    bias_two = 1.0 - 0.999**10
    direction = new_first / bias_one / (jnp.sqrt(new_second / bias_two) + 1e-08)
    update = jnp.dot(direction, basis.T, precision=lax.Precision.HIGHEST)
    return (mixed.astype(jnp.bfloat16), update, new_first, new_second)


def solution(mesh):
    in_specs = (
        P("fsdp", "tp"),
        P("fsdp", "tp"),
        P("fsdp", None),
        P("fsdp", None),
        P("tp", "fsdp"),
        P("tp", "fsdp"),
        P("fsdp", "tp"),
        P(None, "tp", None),
        P("fsdp", None),
        P("fsdp", None),
    )
    out_specs = (P("fsdp", "tp"), P("fsdp", "tp"), P("fsdp", None), P("fsdp", None))
    return jax.shard_map(body, mesh=mesh, in_specs=in_specs, out_specs=out_specs, check_vma=False)
```

profile of v0, /device:TPU:8, one launch (start us, length us, event | category | flops | bytes accessed | tf_op | source)
XLA Modules:
  0.0 443.0 jit_solution(6153673933734960774)
XLA Ops:
  7.2 0.8 convert_reduce_fusion.1
  8.1 0.1 copy.36
  8.2 0.1 reduce_window_sum.11
  8.3 0.7 select_reduce_fusion.1
  9.1 0.7 multiply_add_fusion
  9.7 0.1 fusion.17
  9.8 1.8 convolution_convert_fusion.2
  11.7 1.0 reshape.53
  12.7 0.3 broadcast_in_dim.16
  12.9 102.5 %all_to_all.53 = bf16[64,36,768]{2,1,0:T(8,128)(2,1)} all-to-all(bf16[64,36,768]{2,1,0:T(8,128)(2,1)S(1)} %bitcast.38), channel_id=1, replica_groups=mesh['fsdp'=64,'tp'=4] {'fsdp'}, dimensions={0} | all-to-all | bytes 7077888 | tf_op jit(solution)/shard_map/all_to_all | solution.py:43
  115.4 6.2 %reshape.55 = bf16[2304,768]{1,0:T(8,128)(2,1)} reshape(bf16[64,36,768]{2,1,0:T(8,128)(2,1)} %all_to_all.53) | data formatting | bytes 7077888 | tf_op jit(solution)/shard_map/reshape | solution.py:47
  121.6 2.3 copy.41
  124.0 4.9 %all-to-all-start.2 = ((bf16[768,4,128]{0,2,1:T(8,128)(2,1)}), bf16[768,4,128]{0,2,1:T(8,128)(2,1)}, u32[]{:S(2)}, u32[]{:S(2)}) async-start(bf16[768,4,128]{0,2,1:T(8,128)(2,1)} %bitcast.40), calls=%async_computation.2 | async-start | bytes 1572864 | tf_op jit(solution)/shard_map/all_to_all | solution.py:50
  128.9 2.4 copy.39
  131.3 7.4 %all-to-all-done.2 = bf16[768,4,128]{0,2,1:T(8,128)(2,1)} async-done(((bf16[768,4,128]{0,2,1:T(8,128)(2,1)}), bf16[768,4,128]{0,2,1:T(8,128)(2,1)}, u32[]{:S(2)}, u32[]{:S(2)}) %all-to-all-start.2) | async-done | bytes 786464 | tf_op jit(solution)/shard_map/all_to_all | solution.py:50
  138.7 8.7 %all-to-all-start.1 = ((bf16[768,4,128]{0,2,1:T(8,128)(2,1)}), bf16[768,4,128]{0,2,1:T(8,128)(2,1)}, u32[]{:S(2)}, u32[]{:S(2)}) async-start(bf16[768,4,128]{0,2,1:T(8,128)(2,1)} %bitcast.39), calls=%async_computation.1 | async-start | bytes 1572864 | tf_op jit(solution)/shard_map/all_to_all | solution.py:49
  147.4 0.1 select_reduce_fusion
  147.5 0.9 fusion.1
  148.5 1.0 reshape.58
  149.4 16.4 %all-to-all-done.1 = bf16[768,4,128]{0,2,1:T(8,128)(2,1)} async-done(((bf16[768,4,128]{0,2,1:T(8,128)(2,1)}), bf16[768,4,128]{0,2,1:T(8,128)(2,1)}, u32[]{:S(2)}, u32[]{:S(2)}) %all-to-all-start.1) | async-done | bytes 786464 | tf_op jit(solution)/shard_map/all_to_all | solution.py:49
  165.8 2.2 broadcast_in_dim.19
  168.0 7.3 %all-to-all-start.4 = ((bf16[64,36,768]{2,1,0:T(8,128)(2,1)}), bf16[64,36,768]{2,1,0:T(8,128)(2,1)}, u32[]{:S(2)}, u32[]{:S(2)}) async-start(bf16[64,36,768]{2,1,0:T(8,128)(2,1)} %bitcast.37), calls=%async_computation.4 | async-start | bytes 7864320 | tf_op jit(solution)/shard_map/all_to_all | solution.py:44
  175.3 0.2 all-gather.5.cloned.1.call-start
  175.6 2.3 copy.42
  177.9 2.3 copy.40
  180.2 81.0 %all-gather.3.cloned.1.call-done = bf16[2304,3072]{1,0:T(8,128)(2,1)} async-done(((bf16[2304,768]{1,0:T(8,128)(2,1)}), bf16[2304,3072]{1,0:T(8,128)(2,1)}) %all-gather.3.cloned.1.call-update) | async-done | bytes 14155792 | tf_op jit(solution)/shard_map/all_gather | solution.py:52
  261.2 7.4 %fusion.35 = f32[2304,128]{1,0:T(8,128)S(1)} fusion(bf16[2304,3072]{1,0:T(8,128)(2,1)} %all-gather.3.cloned.1.call-done, bf16[3072,128]{1,0:T(8,128)(2,1)} %bitcast.42), kind=kOutput, calls=%fused_computation.58 | convolution fusion | flops 1811939328 | bytes 16121856 | tf_op jit(solution)/shard_map/dot_general | solution.py:53
  268.6 2.1 copy-done.7
  270.7 4.8 %fusion = bf16[2304,128]{1,0:T(8,128)(2,1)} fusion(bf16[2304,3072]{1,0:T(8,128)(2,1)S(1)} %copy-done.7, bf16[3072,128]{1,0:T(8,128)(2,1)S(1)} %bitcast.41, f32[2304,128]{1,0:T(8,128)S(1)} %fusion.35), kind=kOutput, calls=%fused_computation.5 | convolution fusion | flops 1813708800 | bytes 16711680 | tf_op jit(solution)/shard_map/dot_general | solution.py:54
  275.6 39.5 %all-gather.5.cloned.1.call-done = bf16[2304,512]{1,0:T(8,128)(2,1)} async-done(((bf16[2304,128]{1,0:T(8,128)(2,1)}), bf16[2304,512]{1,0:T(8,128)(2,1)}) %all-gather.5.cloned.1.call-update) | async-done | bytes 2359312 | tf_op jit(solution)/shard_map/all_gather | solution.py:56
  315.1 5.6 %convolution_convert_fusion = bf16[2304,768]{1,0:T(8,128)(2,1)} fusion(bf16[2304,512]{1,0:T(8,128)(2,1)} %all-gather.5.cloned.1.call-done, bf16[512,768]{1,0:T(8,128)(2,1)} %param.16), kind=kOutput, calls=%fused_computation.3 | convolution fusion | flops 1813708800 | bytes 6684672 | tf_op jit(solution)/shard_map/dot_general | solution.py:57
  320.7 6.1 %convert_element_type.34 = bf16[64,36,768]{2,1,0:T(8,128)(2,1)} reshape(bf16[2304,768]{1,0:T(8,128)(2,1)} %convolution_convert_fusion) | data formatting | bytes 7077888 | tf_op jit(solution)/shard_map/convert_element_type | solution.py:62
  326.8 10.7 %all-to-all-start.3 = ((bf16[64,36,768]{2,1,0:T(8,128)(2,1)}), bf16[64,36,768]{2,1,0:T(8,128)(2,1)}, u32[]{:S(2)}, u32[]{:S(2)}) async-start(bf16[64,36,768]{2,1,0:T(8,128)(2,1)} %convert_element_type.34), calls=%async_computation.3 | async-start | bytes 7864320 | tf_op jit(solution)/shard_map/all_to_all | solution.py:61
  337.5 0.3 all-reduce.2.cloned.1.call-start
  337.8 6.2 %reshape.60 = bf16[2304,768]{1,0:T(8,128)(2,1)} reshape(bf16[64,36,768]{2,1,0:T(8,128)(2,1)} %all-to-all-done.4) | data formatting | bytes 7077888 | tf_op jit(solution)/shard_map/reshape | solution.py:46
  343.9 4.8 %fusion.36 = f32[512,768]{1,0:T(8,128)S(1)} fusion(bf16[2304,512]{1,0:T(8,128)(2,1)} %all-gather.5.cloned.1.call-done, bf16[2304,768]{1,0:T(8,128)(2,1)} %reshape.60), kind=kOutput, calls=%fused_computation.59 | convolution fusion | flops 1811939328 | bytes 7471104 | tf_op jit(solution)/shard_map/dot_general | solution.py:58
  348.7 2.2 convolution_convert_fusion.1
  351.0 48.7 %all-reduce.2.cloned.1.call-done = bf16[512,512]{1,0:T(8,128)(2,1)} async-done(((bf16[512,512]{1,0:T(8,128)(2,1)}), bf16[512,512]{1,0:T(8,128)(2,1)}) %all-reduce.2.cloned.1.call-update) | async-done | bytes 524304 | tf_op jit(solution)/shard_map/psum | solution.py:74
  399.7 2.0 fusion.2
  401.8 0.9 copy-done.1
  402.7 0.3 copy-done.2
  403.1 3.1 fusion.4
  406.2 22.0 %all-to-all-done.3 = bf16[64,36,768]{2,1,0:T(8,128)(2,1)} async-done(((bf16[64,36,768]{2,1,0:T(8,128)(2,1)}), bf16[64,36,768]{2,1,0:T(8,128)(2,1)}, u32[]{:S(2)}, u32[]{:S(2)}) %all-to-all-start.3) | async-done | bytes 3538976 | tf_op jit(solution)/shard_map/all_to_all | solution.py:61
  428.1 2.7 convert_reduce_fusion
  430.9 0.9 copy.43
  431.8 1.9 gather_fusion.1
  433.7 1.9 gather_fusion
  435.7 0.7 add_convert_fusion
  (22 shorter events, 0.2 us)
Async XLA Ops:
  7.2 341.6 %copy-start = (bf16[4,768,512]{2,1,0:T(8,128)(2,1)S(1)}, bf16[4,768,512]{2,1,0:T(8,128)(2,1)}, u32[]{:S(2)}) copy-start(bf16[4,768,512]{2,1,0:T(8,128)(2,1)} %param.17) | copy-start | bytes 9437188
  7.2 254.0 %all-gather.3.cloned.1.call-start = ((), (), s32[]{:S(2)}) async-start(), calls=%async_computation.5 | async-start | bytes 17694720 | tf_op jit(solution)/shard_map/all_gather | solution.py:52
  121.6 25.8 %copy-start.6 = (f32[64,2]{0,1:T(2,128)S(1)}, f32[64,2]{0,1:T(2,128)}, u32[]{:S(2)}) copy-start(f32[64,2]{0,1:T(2,128)} %param.13) | copy-start | bytes 1540
  121.6 25.9 %copy-start.4 = (bf16[64,768]{1,0:T(8,128)(2,1)S(1)}, bf16[64,768]{1,0:T(8,128)(2,1)}, u32[]{:S(2)}) copy-start(bf16[64,768]{1,0:T(8,128)(2,1)} %param.11) | copy-start | bytes 294916
  124.0 14.7 %all-to-all-start.2 = ((bf16[768,4,128]{0,2,1:T(8,128)(2,1)}), bf16[768,4,128]{0,2,1:T(8,128)(2,1)}, u32[]{:S(2)}, u32[]{:S(2)}) async-start(bf16[768,4,128]{0,2,1:T(8,128)(2,1)} %bitcast.40), calls=%async_computation.2 | async-start | bytes 1572864 | tf_op jit(solution)/shard_map/all_to_all | solution.py:50
  138.7 27.1 %all-to-all-start.1 = ((bf16[768,4,128]{0,2,1:T(8,128)(2,1)}), bf16[768,4,128]{0,2,1:T(8,128)(2,1)}, u32[]{:S(2)}, u32[]{:S(2)}) async-start(bf16[768,4,128]{0,2,1:T(8,128)(2,1)} %bitcast.39), calls=%async_computation.1 | async-start | bytes 1572864 | tf_op jit(solution)/shard_map/all_to_all | solution.py:49
  168.0 158.8 %all-to-all-start.4 = ((bf16[64,36,768]{2,1,0:T(8,128)(2,1)}), bf16[64,36,768]{2,1,0:T(8,128)(2,1)}, u32[]{:S(2)}, u32[]{:S(2)}) async-start(bf16[64,36,768]{2,1,0:T(8,128)(2,1)} %bitcast.37), calls=%async_computation.4 | async-start | bytes 7864320 | tf_op jit(solution)/shard_map/all_to_all | solution.py:44
  175.3 139.7 %all-gather.5.cloned.1.call-start = ((), (), s32[]{:S(2)}) async-start(), calls=%async_computation.6 | async-start | bytes 2949120 | tf_op jit(solution)/shard_map/all_gather | solution.py:56
  261.2 7.4 %copy-start.3 = (bf16[4,768,128]{2,1,0:T(8,128)(2,1)S(1)}, bf16[4,768,128]{2,1,0:T(8,128)(2,1)}, u32[]{:S(2)}) copy-start(bf16[4,768,128]{2,1,0:T(8,128)(2,1)} %copy.42) | copy-start | bytes 2359300
  261.2 9.5 %copy-start.7 = (bf16[2304,3072]{1,0:T(8,128)(2,1)S(1)}, bf16[2304,3072]{1,0:T(8,128)(2,1)}, u32[]{:S(2)}) copy-start(bf16[2304,3072]{1,0:T(8,128)(2,1)} %all-gather.3.cloned.1.call-done) | copy-start | bytes 42467332
  326.8 101.3 %all-to-all-start.3 = ((bf16[64,36,768]{2,1,0:T(8,128)(2,1)}), bf16[64,36,768]{2,1,0:T(8,128)(2,1)}, u32[]{:S(2)}, u32[]{:S(2)}) async-start(bf16[64,36,768]{2,1,0:T(8,128)(2,1)} %convert_element_type.34), calls=%async_computation.3 | async-start | bytes 7864320 | tf_op jit(solution)/shard_map/all_to_all | solution.py:61
  337.5 62.2 %all-reduce.2.cloned.1.call-start = ((), (), s32[]{:S(2)}) async-start(), calls=%async_computation.7 | async-start | bytes 1048576 | tf_op jit(solution)/shard_map/psum | solution.py:74
  348.7 2.3 copy-start.5
  401.8 1.0 copy-start.1
  401.8 1.3 copy-start.2
Sparse Core Ops, SparseCore 0:
  121.7 139.3 all-gather.2
  275.7 39.3 all-gather.4
  351.1 48.5 all-reduce.1
where the time goes:
time: 445 us; the launch traced here: 443 us
  waiting for transfers between devices  215 us (48%)
  blocking collectives  103 us (23%)
  local copies, waits for them, and re-layouts  40.5 us (9%)
  starting transfers between devices  32.1 us (7%)
  matrix products  30.8 us (7%)
  between operations  14 us (3%)
  other arithmetic  8.03 us (2%)
    all_to_all x1, blocking collectives, body(): lax.all_to_all(send_rows, 'fsdp', split_axis=0, concat_axis=0, tiled=True)  103 us
    all_gather x1, waiting for transfers between devices, body(): piece = lax.all_gather(routed_rows, 'tp', axis=1, tiled=True)  81 us
    psum x1, waiting for transfers between devices, body(): low = lax.psum(low_part.astype(jnp.bfloat16), 'tp').astype(jnp.float32)  48.7 us
    all_gather x1, waiting for transfers between devices, body(): hidden = lax.all_gather(hidden_part, 'tp', axis=1, tiled=True)  39.5 us
    all_to_all x1, waiting for transfers between devices, body(): lax.all_to_all(partial_out.reshape(sources, MOST, features).astype(jnp.bf...  22 us
    all_to_all x1, waiting for transfers between devices, body(): lax.all_to_all(gate_weight, 'tp', split_axis=1, concat_axis=0, tiled=True)  16.4 us
    all_to_all x1, starting transfers between devices, body(): lax.all_to_all(partial_out.reshape(sources, MOST, features).astype(jnp.bf...  10.7 us
  transfers between devices with their start and end apart: 7, of which 6 were waited for; matrix products, arithmetic and copies ran while one was open for 13% of the time, Pallas kernels for 0%

commit v1 on v0

v1 whole, which is shorter than its diff:
```python
import functools

import jax
import jax.numpy as jnp
from jax import lax
from jax.experimental import pallas as pl
from jax.experimental.pallas import tpu as pltpu
from jax.sharding import PartitionSpec as P

EXPERTS = 4
MOST = 36
PAD = 48
ROWS = 4 * MOST
PIECES = 8
RELZ = (0, 1, -1, 2, -2, 3, -3, 4)
LAG1, LAG2, LAG3, LAG4 = 1, 2, 3, 4
MESH = pl.DeviceIdType.MESH
F32, BF16 = jnp.float32, jnp.bfloat16


def dot(a, b):
    return jnp.dot(a, b, preferred_element_type=F32)


def dot_t(a, b):
    return lax.dot_general(a, b, (((0,), (0,)), ((), ())), preferred_element_type=F32)


def moe_kernel(
    ids_ref, route_ref, tok_ref, cot_ref, wg_hbm, wu_hbm, wd_hbm, proj_hbm,
    mixed_ref, low_ref,
    wg, wu, wd, proj, pick_s, slotw_s, xs, sps, spr, spz, zb, zs, xb, spb,
    p2, pr, pll, qa, po, ra, rb, fl, fr, hd, out, cb, eb, rbk, lowt, lc, lr, lo,
    lsem, wsend, wrecv, zsend, zrecv, zssend, zsrecv, sysend, syrecv, sxsend, sxrecv,
    xsend, xrecv, xfsend, xfrecv, ysend, yrecv, csend, crecv, rsend, rrecv, lcsend, lcrecv, losend, lorecv,
):
    f = lax.axis_index("fsdp")
    y = lax.axis_index("tp")
    z, x, c = f // 8, (f // 2) % 4, f % 2
    yr, yl, yo = (y + 1) % 4, (y + 3) % 4, (y + 2) % 4

    def at_y(yy):
        return (f, yy)

    def at_x(step):
        return (z * 8 + ((x + step) % 4) * 2 + c, y)

    def at_z(zz):
        return (zz * 8 + x * 2 + c, y)

    sibling = (z * 8 + x * 2 + (1 - c), y)

    def rcopy(src, dst, send, recv, dev):
        return pltpu.make_async_remote_copy(
            src_ref=src, dst_ref=dst, send_sem=send, recv_sem=recv, device_id=dev, device_id_type=MESH
        )

    local = []
    for k in range(2):
        cols = pl.ds(k * 256, 256)
        local.append(pltpu.make_async_copy(wg_hbm.at[:, cols], wg.at[2 * c + k], lsem.at[k]))
        local.append(pltpu.make_async_copy(wu_hbm.at[:, cols], wu.at[2 * c + k], lsem.at[2 + k]))
    local.append(pltpu.make_async_copy(wd_hbm, wd.at[c], lsem.at[4]))
    local.append(pltpu.make_async_copy(proj_hbm, proj, lsem.at[5]))
    for cp in local:
        cp.start()

    barrier = pltpu.get_barrier_semaphore()
    partners = [at_y(yr), at_y(yl), at_y(yo), at_x(1), at_x(3), at_x(2), sibling]
    partners += [at_z((z + k) % 8) for k in range(1, 8)]
    for dev in partners:
        pl.semaphore_signal(barrier, inc=1, device_id=dev, device_id_type=MESH)

    slot = lax.broadcasted_iota(jnp.int32, (EXPERTS * PAD, 64), 0)
    slot_e = (slot >= PAD).astype(jnp.int32) + (slot >= 2 * PAD).astype(jnp.int32) + (slot >= 3 * PAD).astype(jnp.int32)
    slot_j = slot - PAD * slot_e
    named0 = (ids_ref[0:1, :] == slot_e).astype(F32)
    named1 = (ids_ref[1:2, :] == slot_e).astype(F32)
    named = named0 + named1
    earlier = (
        lax.broadcasted_iota(jnp.int32, (64, 64), 0) < lax.broadcasted_iota(jnp.int32, (64, 64), 1)
    ).astype(F32)
    before = dot(named.astype(BF16), earlier.astype(BF16))
    pick = jnp.where(before == slot_j.astype(F32), named, 0.0)
    slot_w = jnp.sum(pick * (named0 * route_ref[0:1, :] + named1 * route_ref[1:2, :]), axis=1, keepdims=True)
    pick = pick.astype(BF16)
    pick_s[...] = pick
    slotw_s[...] = slot_w
    rows = dot(pick, tok_ref[...]).astype(BF16)
    xs[...] = rows.reshape(EXPERTS, PAD, 768)

    pl.semaphore_wait(barrier, len(partners))

    remote = []
    for k in range(2):
        cols = pl.ds(k * 256, 256)
        remote.append((wg_hbm.at[:, cols], wg, 2 * c + k, 2 * (1 - c) + k))
        remote.append((wu_hbm.at[:, cols], wu, 2 * c + k, 2 * (1 - c) + k))
    remote.append((wd_hbm, wd, c, 1 - c))
    wcopies = [rcopy(s, d.at[mine], wsend.at[n], wrecv.at[n], sibling) for n, (s, d, mine, _) in enumerate(remote)]
    wwaits = [rcopy(s, d.at[theirs], wsend.at[n], wrecv.at[n], sibling) for n, (s, d, _, theirs) in enumerate(remote)]

    def zcopy(k):
        there = (z + 8 - RELZ[k]) % 8
        return rcopy(xs.at[there // 2], zb.at[k // 4, k % 4], zsend.at[k], zrecv.at[k], at_z(there))

    def zscopy(k):
        there = (z + 8 - RELZ[k]) % 8
        return rcopy(spz.at[there // 2], zs.at[k // 4, k % 4], zssend.at[k], zsrecv.at[k], at_z(there))

    for k in range(1, 8):
        zcopy(k).start()
    for cp in wcopies:
        cp.start()
    zb[0, 0] = xs[z // 2]

    local[5].wait()
    scaled = (dot(pick, cot_ref[...]) * slot_w).astype(BF16)
    for e in range(EXPERTS):
        part = dot(scaled[e * PAD:(e + 1) * PAD], proj[e]).astype(BF16)
        for d in range(4):
            sps[d, e * PAD:(e + 1) * PAD, :] = part[:, d * 128:(d + 1) * 128]
    sycopies = [
        rcopy(sps.at[d], spr.at[k], sysend.at[k], syrecv.at[k], at_y(d)) for k, d in enumerate((yr, yl, yo))
    ]
    for cp in sycopies:
        cp.start()

    def squeeze():
        r = lax.broadcasted_iota(jnp.int32, (ROWS, 4 * PAD), 0)
        col = lax.broadcasted_iota(jnp.int32, (ROWS, 4 * PAD), 1)
        src = (r >= MOST).astype(jnp.int32) + (r >= 2 * MOST).astype(jnp.int32) + (r >= 3 * MOST).astype(jnp.int32)
        return (col == r + (PAD - MOST) * src).astype(F32).astype(BF16)

    def widen():
        r = lax.broadcasted_iota(jnp.int32, (4 * PAD, ROWS), 1)
        col = lax.broadcasted_iota(jnp.int32, (4 * PAD, ROWS), 0)
        src = (r >= MOST).astype(jnp.int32) + (r >= 2 * MOST).astype(jnp.int32) + (r >= 3 * MOST).astype(jnp.int32)
        return (col == r + (PAD - MOST) * src).astype(F32).astype(BF16)

    def xcopy(h, r):
        return rcopy(xb.at[4 * h], xb.at[4 * h + r], xsend.at[4 * h + r], xrecv.at[4 * h + r], at_x(1 if r == 2 else 3))

    def xforward(h, r):
        if r == 2:
            return rcopy(xb.at[4 * h + 2, 0], xb.at[4 * h + 3, 0], xfsend.at[h, 0], xfrecv.at[h, 0], at_x(1))
        return rcopy(xb.at[4 * h + 1, 1], xb.at[4 * h + 3, 1], xfsend.at[h, 1], xfrecv.at[h, 1], at_x(3))

    def gather_rows(h):
        for k in range(4 * h, 4 * h + 4):
            if k:
                zcopy(k).wait_recv()
        dense = dot(squeeze(), zb[h].reshape(4 * PAD, 768)).astype(BF16)
        xb[4 * h, 0] = dense[:, :384]
        xb[4 * h, 1] = dense[:, 384:]
        xcopy(h, 2).start()
        xcopy(h, 1).start()

    def sxcopy(k):
        return rcopy(spb.at[0], spb.at[(2, 1, 3)[k]], sxsend.at[k], sxrecv.at[k], at_x((1, 3, 2)[k]))

    gather_rows(0)
    for cp in local[:5]:
        cp.wait()
    for cp in wwaits[:4]:
        cp.wait_recv()

    def ycopy(kind, i):
        src, dst, dev = {
            0: lambda: (p2.at[i, 0], ra.at[i], yr),
            1: lambda: (p2.at[i, 1], rb.at[i], yl),
            2: lambda: (pr.at[i, 1], fl.at[i, 1], yr),
            3: lambda: (pll.at[i, 0], fr.at[i, 0], yl),
            4: lambda: (pr.at[i, 0], fl.at[i, 0], yr),
            5: lambda: (pll.at[i, 1], fr.at[i, 1], yl),
            6: lambda: (hd.at[i, y], hd.at[i, y], yr),
            7: lambda: (hd.at[i, y], hd.at[i, y], yl),
            8: lambda: (hd.at[i, yl, 0], hd.at[i, yl, 0], yr),
            9: lambda: (hd.at[i, yr, 1], hd.at[i, yr, 1], yl),
        }[kind]()
        return rcopy(src, dst, ysend.at[kind, i], yrecv.at[kind, i], at_y(dev))

    def yarrive(kind, i):
        if kind < 6:
            ycopy(kind, i).wait_recv()
            return
        dst = {
            6: lambda: hd.at[i, yl],
            7: lambda: hd.at[i, yr],
            8: lambda: hd.at[i, yo, 0],
            9: lambda: hd.at[i, yo, 1],
        }[kind]()
        rcopy(dst, dst, ysend.at[kind, i], yrecv.at[kind, i], at_y(yr)).wait_recv()

    def stage0(i):
        h, r = i // 4, i % 4

        @pl.when(r == 1)
        def _():
            xcopy_wait(i)
            xforward(h, 1).start()

        @pl.when(r == 2)
        def _():
            xcopy_wait(i)
            xforward(h, 2).start()

        @pl.when(r == 3)
        def _():
            xforward(h, 2).wait_recv()
            xforward(h, 1).wait_recv()

        v = jnp.concatenate([xb[i, 0], xb[i, 1]], axis=1)
        p2[i, 0] = dot(v, wg[yo]).astype(BF16)
        ycopy(0, i).start()
        p2[i, 1] = dot(v, wu[yo]).astype(BF16)
        ycopy(1, i).start()
        pr[i, 1] = dot(v, wu[yr]).astype(BF16)
        ycopy(2, i).start()
        pll[i, 0] = dot(v, wg[yl]).astype(BF16)
        ycopy(3, i).start()
        qa[i, 0] = dot(v, wg[yr])
        qa[i, 1] = dot(v, wu[yl])
        po[i, 0] = dot(v, wg[y])
        po[i, 1] = dot(v, wu[y])

    def xcopy_wait(i):
        rcopy(xb.at[i], xb.at[i], xsend.at[i], xrecv.at[i], at_x(1)).wait_recv()

    def stage1(i):
        yarrive(0, i)
        pr[i, 0] = (qa[i, 0] + ra[i].astype(F32)).astype(BF16)
        ycopy(4, i).start()
        yarrive(1, i)
        pll[i, 1] = (qa[i, 1] + rb[i].astype(F32)).astype(BF16)
        ycopy(5, i).start()

    def stage2(i):
        for kind in (2, 3, 4, 5):
            yarrive(kind, i)
        g = po[i, 0] + fl[i, 0].astype(F32) + fr[i, 0].astype(F32)
        u = po[i, 1] + fl[i, 1].astype(F32) + fr[i, 1].astype(F32)
        hidden = (g / (1.0 + jnp.exp(-g)) * u).astype(BF16)
        hd[i, y, 0] = hidden[:, :128]
        hd[i, y, 1] = hidden[:, 128:]
        ycopy(6, i).start()
        ycopy(7, i).start()

    def stage3(i):
        yarrive(6, i)
        ycopy(8, i).start()
        yarrive(7, i)
        ycopy(9, i).start()

    def ccopy(i):
        h, r = i // 4, i % 4
        step = jnp.where(r == 1, 1, jnp.where(r == 2, 3, 2))
        there = 4 * h + jnp.where(r == 3, 3, 3 - r)
        return rcopy(out.at[i], cb.at[there], csend.at[i], crecv.at[there], at_x(step))

    def carrive(i):
        return rcopy(cb.at[i], cb.at[i], csend.at[i], crecv.at[i], at_x(1))

    def stage4(i):
        h, r = i // 4, i % 4
        yarrive(8, i)
        yarrive(9, i)
        hidden = jnp.concatenate([hd[i, d, k] for d in range(4) for k in range(2)], axis=1)
        out[i] = dot(hidden, wd[...].reshape(1024, 768)).astype(BF16)

        @pl.when(r > 0)
        def _():
            ccopy(i).start()

        lowt[...] += dot_t(spb[r, h], hidden)

    def rcopy_back(k):
        there = (z + 8 + RELZ[k]) % 8
        return rcopy(eb.at[k // 4, k % 4], rbk.at[z % 2, z // 2], rsend.at[k], rrecv.at[k], at_z(there))

    def rarrive(k):
        come = (z + 8 - RELZ[k]) % 8
        dst = rbk.at[come % 2, come // 2]
        return rcopy(dst, dst, rsend.at[k], rrecv.at[k], at_z((z + 1) % 8))

    def combine(h):
        for r in range(1, 4):
            carrive(4 * h + r).wait_recv()
        total = out[4 * h].astype(F32)
        for r in range(1, 4):
            total = total + cb[4 * h + r].astype(F32)
        wide = dot(widen(), total.astype(BF16)).astype(BF16)
        eb[h] = wide.reshape(4, PAD, 768)
        for k in range(4 * h, 4 * h + 4):
            if k:
                rcopy_back(k).start()
            else:
                rbk[z % 2, z // 2] = eb[0, 0]

    lowt[...] = jnp.zeros_like(lowt)

    def step(it, carry):
        @pl.when(it == 1)
        def _():
            for cp in sycopies:
                cp.wait_recv()
            total = sps[y].astype(F32)
            for k in range(3):
                total = total + spr[k].astype(F32)
            spz[...] = total.astype(BF16).reshape(EXPERTS, PAD, 128)
            for k in range(1, 8):
                zscopy(k).start()
            zs[0, 0] = spz[z // 2]

        @pl.when(it == 2)
        def _():
            gather_rows(1)

        @pl.when(it == 3)
        def _():
            for k in range(1, 8):
                zscopy(k).wait_recv()
            for h in range(2):
                spb[0, h] = dot(squeeze(), zs[h].reshape(4 * PAD, 128)).astype(BF16)
            for k in range(3):
                sxcopy(k).start()

        def run(stage, lag):
            @pl.when((it >= lag) & (it < lag + PIECES))
            def _():
                stage(it - lag)

        run(stage3, LAG3)
        run(stage2, LAG2)
        run(stage1, LAG1)
        run(stage0, 0)

        @pl.when(it == LAG4)
        def _():
            for k in range(3):
                sxcopy(k).wait_recv()
            wwaits[4].wait_recv()

        run(stage4, LAG4)

        @pl.when(it == LAG4 + 5)
        def _():
            combine(0)

        return carry

    lax.fori_loop(0, PIECES + LAG4, step, 0)

    lc[...] = lowt[...].T.reshape(2, 512, 128)
    lcc = rcopy(lc.at[1 - c], lr, lcsend, lcrecv, sibling)
    lcc.start()
    combine(1)
    lcc.wait_recv()
    lo[y] = (lc[c] + lr[...]).astype(BF16)
    locopies = [rcopy(lo.at[y], lo.at[y], losend.at[k], lorecv.at[k], at_y(d)) for k, d in enumerate((yr, yl, yo))]
    lowaits = [rcopy(lo.at[d], lo.at[d], losend.at[k], lorecv.at[k], at_y(yr)) for k, d in enumerate((yl, yr, yo))]
    for cp in locopies:
        cp.start()
    for cp in lowaits:
        cp.wait_recv()
    low_ref[...] = lo[...]
    for k in range(1, 8):
        rarrive(k).wait_recv()
    back = (rbk[0].astype(F32) + rbk[1].astype(F32)).reshape(EXPERTS * PAD, 768) * slotw_s[...]
    high = back.astype(BF16)
    rest = (back - high.astype(F32)).astype(BF16)
    mixed_ref[...] = (dot_t(pick_s[...], high) + dot_t(pick_s[...], rest)).astype(BF16)

    for k in range(1, 8):
        zcopy(k).wait_send()
        zscopy(k).wait_send()
        rcopy_back(k).wait_send()
    for cp in wcopies + sycopies + locopies + [lcc]:
        cp.wait_send()
    for k in range(3):
        sxcopy(k).wait_send()
    for h in range(2):
        for r in (1, 2):
            xcopy(h, r).wait_send()
            xforward(h, r).wait_send()

    def drain(i, carry):
        for kind in range(10):
            ycopy(kind, i).wait_send()

        @pl.when(i % 4 > 0)
        def _():
            ccopy(i).wait_send()

        return carry

    lax.fori_loop(0, PIECES, drain, 0)


def moe(ids, route, tokens, cotangent, gate, up, down, projector):
    vm = lambda *shape: pltpu.VMEM(shape, BF16)
    vf = lambda *shape: pltpu.VMEM(shape, F32)
    sem = lambda *shape: pltpu.SemaphoreType.DMA(shape)
    n = PIECES
    scratch = [
        vm(4, 768, 256), vm(4, 768, 256), vm(2, 512, 768), vm(4, 768, 512),
        vm(192, 64), vf(192, 1), vm(4, PAD, 768), vm(4, 192, 128), vm(3, 192, 128), vm(4, PAD, 128),
        vm(2, 4, PAD, 768), vm(2, 4, PAD, 128), vm(n, 2, ROWS, 384), vm(4, 2, ROWS, 128),
        vm(n, 2, ROWS, 256), vm(n, 2, ROWS, 256), vm(n, 2, ROWS, 256), vf(n, 2, ROWS, 256), vf(n, 2, ROWS, 256),
        vm(n, ROWS, 256), vm(n, ROWS, 256), vm(n, 2, ROWS, 256), vm(n, 2, ROWS, 256),
        vm(n, 4, 2, ROWS, 128), vm(n, ROWS, 768), vm(n, ROWS, 768), vm(2, 4, PAD, 768), vm(2, 4, PAD, 768),
        vf(128, 1024), vf(2, 512, 128), vf(512, 128), vm(4, 512, 128),
        sem(6), sem(5), sem(5), sem(8), sem(8), sem(8), sem(8), sem(3), sem(3), sem(3), sem(3),
        sem(8), sem(8), sem(2, 2), sem(2, 2), sem(10, n), sem(10, n), sem(8), sem(8), sem(8), sem(8),
        pltpu.SemaphoreType.DMA, pltpu.SemaphoreType.DMA, sem(3), sem(3),
    ]
    vmem = pl.BlockSpec(memory_space=pltpu.VMEM)
    hbm = pl.BlockSpec(memory_space=pl.ANY)
    return pl.pallas_call(
        moe_kernel,
        out_shape=(
            jax.ShapeDtypeStruct((64, 768), BF16),
            jax.ShapeDtypeStruct((4, 512, 128), BF16),
        ),
        in_specs=[vmem, vmem, vmem, vmem, hbm, hbm, hbm, hbm],
        out_specs=(vmem, vmem),
        scratch_shapes=scratch,
        compiler_params=pltpu.CompilerParams(
            collective_id=0, has_side_effects=True, vmem_limit_bytes=52 * 1024 * 1024
        ),
        cost_estimate=pl.CostEstimate(flops=8_000_000_000, bytes_accessed=6_000_000, transcendentals=300_000),
        name="moe",
    )(ids, route, tokens, cotangent, gate, up, down, projector)


def update_kernel(expert_ref, low_ref, first_ref, second_ref, proj_ref, update_ref, new_first_ref, new_second_ref):
    low = jnp.concatenate([low_ref[d] for d in range(4)], axis=1).astype(F32)
    new_first = 0.9 * first_ref[...] + 0.1 * low
    new_second = 0.999 * second_ref[...] + 0.001 * low * low
    new_first_ref[...] = new_first
    new_second_ref[...] = new_second
    bias_one = 1.0 - 0.9**10
    bias_two = 1.0 - 0.999**10
    direction = new_first / bias_one / (jnp.sqrt(new_second / bias_two) + 1e-08)
    high = direction.astype(BF16)
    rest = (direction - high.astype(F32)).astype(BF16)
    basis = proj_ref[0]
    dims = (((1,), (1,)), ((), ()))
    update_ref[...] = lax.dot_general(high, basis, dims, preferred_element_type=F32) + lax.dot_general(
        rest, basis, dims, preferred_element_type=F32
    )


def update_step(expert, low, first, second, projector):
    rows = 128
    return pl.pallas_call(
        update_kernel,
        out_shape=(
            jax.ShapeDtypeStruct((512, 768), F32),
            jax.ShapeDtypeStruct((512, 512), F32),
            jax.ShapeDtypeStruct((512, 512), F32),
        ),
        grid_spec=pltpu.PrefetchScalarGridSpec(
            num_scalar_prefetch=1,
            grid=(512 // rows,),
            in_specs=[
                pl.BlockSpec((4, rows, 128), lambda i, e: (0, i, 0)),
                pl.BlockSpec((rows, 512), lambda i, e: (i, 0)),
                pl.BlockSpec((rows, 512), lambda i, e: (i, 0)),
                pl.BlockSpec((1, 768, 512), lambda i, e: (e[0], 0, 0)),
            ],
            out_specs=(
                pl.BlockSpec((rows, 768), lambda i, e: (i, 0)),
                pl.BlockSpec((rows, 512), lambda i, e: (i, 0)),
                pl.BlockSpec((rows, 512), lambda i, e: (i, 0)),
            ),
        ),
        cost_estimate=pl.CostEstimate(flops=800_000_000, bytes_accessed=7_000_000, transcendentals=300_000),
        name="update",
    )(expert, low, first, second, projector)


def body(
    tokens,
    cotangent,
    expert_ids,
    route_weights,
    gate_weight,
    up_weight,
    down_weight,
    projector,
    first_moment,
    second_moment,
):
    mixed, low = moe(
        expert_ids.T, route_weights.T, tokens, cotangent, gate_weight, up_weight, down_weight, projector
    )
    expert = (lax.axis_index("fsdp") // 16).astype(jnp.int32).reshape(1)
    update, new_first, new_second = update_step(expert, low, first_moment, second_moment, projector)
    return mixed, update, new_first, new_second


def solution(mesh):
    in_specs = (
        P("fsdp", "tp"),
        P("fsdp", "tp"),
        P("fsdp", None),
        P("fsdp", None),
        P("tp", "fsdp"),
        P("tp", "fsdp"),
        P("fsdp", "tp"),
        P(None, "tp", None),
        P("fsdp", None),
        P("fsdp", None),
    )
    out_specs = (P("fsdp", "tp"), P("fsdp", "tp"), P("fsdp", None), P("fsdp", None))
    return jax.shard_map(body, mesh=mesh, in_specs=in_specs, out_specs=out_specs, check_vma=False)
```

time: 445 us -> 113 us (0.25)
  waiting for transfers between devices: 215 us -> 0 us
  Pallas kernels: 0 us -> 105 us
  blocking collectives: 103 us -> 0 us
  local copies, waits for them, and re-layouts: 40.5 us -> 5.69 us
  starting transfers between devices: 32.1 us -> 0 us
  matrix products: 30.8 us -> 0 us
  between operations: 14 us -> 0.68 us
  other arithmetic: 8.03 us -> 0 us
    all_gather x2 -> x0, waiting for transfers between devices: 121 us -> none  [the longest x1 81 us: body(): piece = lax.all_gather(routed_rows, 'tp', axis=1, tiled=True)]
    pallas_call x0 -> x2, Pallas kernels: none -> 105 us  [the longest x1 98.9 us: moe(): pl.pallas_call(moe_kernel, out_shape=(jax.ShapeDtypeStruct((64, 768), BF1...]
    all_to_all x1 -> x0, blocking collectives: 103 us -> none  [body(): lax.all_to_all(send_rows, 'fsdp', split_axis=0, concat_axis=0, tiled=True)]
    psum x1 -> x0, waiting for transfers between devices: 48.7 us -> none  [body(): low = lax.psum(low_part.astype(jnp.bfloat16), 'tp').astype(jnp.float32)]
    all_to_all x4 -> x0, waiting for transfers between devices: 45.8 us -> none  [the longest x1 22 us: body(): lax.all_to_all(partial_out.reshape(sources, MOST, features).astype(jnp.bf...]
    all_to_all x4 -> x0, starting transfers between devices: 31.6 us -> none  [the longest x1 10.7 us: body(): lax.all_to_all(partial_out.reshape(sources, MOST, features).astype(jnp.bf...]
    dot_general x8 -> x0, matrix products: 30.8 us -> none  [the longest x1 7.42 us: body(): gate_part = jnp.dot(piece, gate_cols, preferred_element_type=jnp.float32)]
    reshape x4 -> x0, local copies, waits for them, and re-layouts: 14.3 us -> none  [the longest x1 6.17 us: body(): routed_grads = got_grads.reshape(sources * MOST, features)]
  transfers between devices with their start and end apart: 7 -> 0, of which waited for: 6 -> 0; matrix products, arithmetic and copies ran while one was open for 13% -> 0% of each run, Pallas kernels for 0% -> 0%
where the time goes in v1:
time: 113 us; the launch traced here: 111 us
  Pallas kernels  105 us (93%)
  local copies, waits for them, and re-layouts  5.69 us (5%)
    pallas_call x1, Pallas kernels, moe(): pl.pallas_call(moe_kernel, out_shape=(jax.ShapeDtypeStruct((64, 768), BF1...  98.9 us
    unnamed x13, local copies, waits for them, and re-layouts  5.69 us
    pallas_call x1, Pallas kernels, update_step(): pl.pallas_call(update_kernel, out_shape=(jax.ShapeDtypeStruct((512, 768),...  5.58 us

profile of v1, /device:TPU:8, one launch (start us, length us, event | category | flops | bytes accessed | tf_op | source)
XLA Modules:
  0.0 110.9 jit_solution(6795192008650489086)
XLA Ops:
  0.6 0.0 copy-start.1
  0.7 1.1 %copy-done.1 = bf16[768,512]{1,0:T(8,128)(2,1)S(1)} copy-done((bf16[768,512]{1,0:T(8,128)(2,1)S(1)}, bf16[768,512]{1,0:T(8,128)(2,1)}, u32[]{:S(2)}) %copy-start.1) | copy-done | bytes 786456
  1.8 0.0 copy-start.2
  1.8 0.9 copy-done.2
  2.7 0.0 copy-start.3
  2.7 0.9 copy-done.3
  3.6 0.0 copy-start.4
  3.6 0.7 copy-done.4
  4.2 0.0 copy-start.5
  4.3 0.7 copy-done.5
  4.9 98.9 %moe.1 = (bf16[64,768]{1,0:T(8,128)(2,1)S(1)}, bf16[4,512,128]{2,1,0:T(8,128)(2,1)S(1)}) custom-call(s32[2,64]{1,0:T(2,128)S(1)} %bitcast.3, f32[2,64]{1,0:T(2,128)S(1)} %bitcast.4, bf16[64,768]{1,0:T(8,128)(2,1)S(1)} %copy-done.2, bf16[64,768]{1,0:T(8,128)(2,1)S(1)} %copy-done.3, bf16[768,512]{1,0:T(8,128)(2,1)S(1)} %copy-done.1, bf16[768,512]{1,0:T(8,128)(2,1)} %wu_hbm.1, ...), custom_call_target="tpu_custom_call" | custom-call | flops 8000000000 | bytes 6000000 | tf_op jit(solution)/shard_map/moe/pallas_call | solution.py:419
  103.9 0.0 copy-start
  103.9 0.8 copy-done
  104.7 5.6 %update.1 = (f32[512,768]{1,0:T(8,128)}, f32[512,512]{1,0:T(8,128)}, f32[512,512]{1,0:T(8,128)}) custom-call(s32[1]{0:T(128)} %bitcast.2.expert_ref, bf16[4,512,128]{2,1,0:T(8,128)(2,1)} %copy-done, f32[512,512]{1,0:T(8,128)} %first_ref.1, f32[512,512]{1,0:T(8,128)} %second_ref.1, bf16[4,768,512]{2,1,0:T(8,128)(2,1)} %proj_ref.1), custom_call_target="tpu_custom_call" | custom-call | flops 800000000 | bytes 7000000 | tf_op jit(solution)/shard_map/update/pallas_call | solution.py:456
  110.2 0.6 copy.15
Async XLA Ops:
  0.6 1.1 %copy-start.1 = (bf16[768,512]{1,0:T(8,128)(2,1)S(1)}, bf16[768,512]{1,0:T(8,128)(2,1)}, u32[]{:S(2)}) copy-start(bf16[768,512]{1,0:T(8,128)(2,1)} %wg_hbm.1) | copy-start | bytes 2359300
  1.8 0.9 copy-start.2
  2.7 0.9 copy-start.3
  3.6 0.7 copy-start.4
  4.2 0.7 copy-start.5
  103.9 0.8 copy-start

commit v2 on v1

v2 whole, which is shorter than its diff:
```python
import jax
import jax.numpy as jnp
from jax import lax
from jax.experimental import pallas as pl
from jax.experimental.pallas import tpu as pltpu
from jax.sharding import PartitionSpec as P

EXPERTS = 4
MOST = 36
MAIN, REST, BLOCK = 32, 16, 112
PAD = MAIN + REST
ROWS = 4 * MOST
PIECES = 8
RELZ = (0, 1, 2, 3, 4, -3, -2, -1)
LAG1, LAG2, LAG3, LAG4, LAG5 = 1, 2, 3, 4, 5
MESH = pl.DeviceIdType.MESH
F32, BF16 = jnp.float32, jnp.bfloat16


def dot(a, b):
    return jnp.dot(a, b, preferred_element_type=F32)


def dot_t(a, b):
    return lax.dot_general(a, b, (((0,), (0,)), ((), ())), preferred_element_type=F32)


def reach(v, size):
    return sum((v >= n * size).astype(jnp.int32) for n in range(1, 4))


def row_of(j, q):
    folded = jnp.where((j >= MAIN + 4 * q) & (j < MAIN + 4 * q + 4), j - 4 * q, -1)
    return jnp.where(j < MAIN, j, folded)


def matcher(shape, dense, q):
    d = lax.broadcasted_iota(jnp.int32, shape, dense)
    w = lax.broadcasted_iota(jnp.int32, shape, 1 - dense)
    ds, ws = reach(d, MOST), reach(w, PAD)
    return ((ds == ws) & (d - MOST * ds == row_of(w - PAD * ws, q))).astype(F32).astype(BF16)


def moe_kernel(
    ids_hbm, route_hbm, tok_hbm, cot_hbm, wg_hbm, wu_hbm, wd_hbm, proj_hbm,
    mixed_ref, low_ref,
    ids_ref, route_ref, tok_ref, cot_ref,
    wg, wu, wd, proj, pick_s, slotw_s, squeeze, widen, xs, xz, sps, spr, spz, sz,
    p2, pr, pll, qa, po, ra, rb, fl, fr, hd, ob, cb, eb, rbk, lowt, lc, lr, lo,
    lsem, wsend, wrecv, zsend, zrecv, zssend, zsrecv, sysend, syrecv, sxsend, sxrecv,
    xsend, xrecv, ysend, yrecv, csend, crecv, rsend, rrecv, lcsend, lcrecv, losend, lorecv,
):
    f = lax.axis_index("fsdp")
    y = lax.axis_index("tp")
    z, x, c = f // 8, (f // 2) % 4, f % 2
    yr, yl, yo = (y + 1) % 4, (y + 3) % 4, (y + 2) % 4

    def at_y(yy):
        return (f, yy)

    def at_x(step):
        return (z * 8 + ((x + step) % 4) * 2 + c, y)

    def at_z(zz):
        return (zz * 8 + x * 2 + c, y)

    def plane(k, sign):
        rel = jnp.where(k < 5, k, k - 8)
        return (z + 8 + sign * rel) % 8

    sibling = (z * 8 + x * 2 + (1 - c), y)

    def rcopy(src, dst, send, recv, dev):
        return pltpu.make_async_remote_copy(
            src_ref=src, dst_ref=dst, send_sem=send, recv_sem=recv, device_id=dev, device_id_type=MESH
        )

    inputs = [
        pltpu.make_async_copy(s, d, lsem.at[n])
        for n, (s, d) in enumerate(((ids_hbm, ids_ref), (route_hbm, route_ref), (tok_hbm, tok_ref), (cot_hbm, cot_ref)))
    ]
    weights = []
    for k in range(2):
        cols = pl.ds(k * 256, 256)
        weights.append(pltpu.make_async_copy(wg_hbm.at[:, cols], wg.at[2 * c + k], lsem.at[4 + k]))
        weights.append(pltpu.make_async_copy(wu_hbm.at[:, cols], wu.at[2 * c + k], lsem.at[6 + k]))
    down_copy = pltpu.make_async_copy(wd_hbm, wd.at[c], lsem.at[8])
    proj_copy = pltpu.make_async_copy(proj_hbm, proj, lsem.at[9])
    for cp in inputs + weights + [proj_copy, down_copy]:
        cp.start()

    barrier = pltpu.get_barrier_semaphore()
    partners = [at_y(yr), at_y(yl), at_y(yo), at_x(1), at_x(3), at_x(2), sibling]
    partners += [at_z((z + k) % 8) for k in range(1, 8)]
    for dev in partners:
        pl.semaphore_signal(barrier, inc=1, device_id=dev, device_id_type=MESH)

    place = lax.broadcasted_iota(jnp.int32, (EXPERTS * PAD, 64), 0)
    place_e = reach(place, PAD)
    place_j = place - PAD * place_e
    earlier = (
        lax.broadcasted_iota(jnp.int32, (64, 64), 0) < lax.broadcasted_iota(jnp.int32, (64, 64), 1)
    ).astype(F32)
    for cp in inputs:
        cp.wait()
    named0 = (ids_ref[0:1, :] == place_e).astype(F32)
    named1 = (ids_ref[1:2, :] == place_e).astype(F32)
    named = named0 + named1
    weight = named0 * route_ref[0:1, :] + named1 * route_ref[1:2, :]
    before = dot(named.astype(BF16), earlier.astype(BF16))
    tail = 0.0
    for q in range(3):
        pick = jnp.where(before == row_of(place_j, q).astype(F32), named, 0.0)
        slotw_s[q] = jnp.sum(pick * weight, axis=1, keepdims=True)
        pick_s[q] = pick.astype(BF16)
        rows = dot(pick.astype(BF16), tok_ref[:, q * 256:(q + 1) * 256])
        rows = rows.reshape(EXPERTS, PAD, 256)
        xs[:, q * MAIN:(q + 1) * MAIN, :] = rows[:, :MAIN].astype(BF16)
        tail = tail + rows[:, MAIN:]
    xs[:, 3 * MAIN:, :] = tail.astype(BF16)

    pl.semaphore_wait(barrier, len(partners))

    def zcopy(k):
        there = plane(k, -1)
        return rcopy(xs.at[there // 2], xz.at[k, 0], zsend.at[k], zrecv.at[k], at_z(there))

    def xcopy(k, r):
        return rcopy(xz.at[k, 0], xz.at[k, r], xsend.at[r, k], xrecv.at[r, k], at_x({2: 1, 1: 3, 3: 2}[r]))

    def spread(k):
        for r in (2, 1, 3):
            xcopy(k, r).start()

    xz[0, 0] = xs[z // 2]
    spread(0)
    for k in range(1, PIECES):
        zcopy(k).start()

    remote = []
    for k in range(2):
        cols = pl.ds(k * 256, 256)
        remote.append((wg_hbm.at[:, cols], wg, 2 * c + k, 2 * (1 - c) + k))
        remote.append((wu_hbm.at[:, cols], wu, 2 * c + k, 2 * (1 - c) + k))
    remote.append((wd_hbm, wd, c, 1 - c))
    wcopies = [rcopy(s, d.at[mine], wsend.at[n], wrecv.at[n], sibling) for n, (s, d, mine, _) in enumerate(remote)]
    wwaits = [rcopy(s, d.at[theirs], wsend.at[n], wrecv.at[n], sibling) for n, (s, d, _, theirs) in enumerate(remote)]
    for cp in wcopies:
        cp.start()

    for q in range(3):
        squeeze[q] = matcher((ROWS, 4 * PAD), 0, q)
        widen[q] = matcher((4 * PAD, ROWS), 1, q)
    lowt[...] = jnp.zeros_like(lowt)

    def zscopy(k):
        there = plane(k, -1)
        return rcopy(spz.at[there // 2], sz.at[0, k], zssend.at[k], zsrecv.at[k], at_z(there))

    sycopies = [
        rcopy(sps.at[d], spr.at[k], sysend.at[k], syrecv.at[k], at_y(d)) for k, d in enumerate((yr, yl, yo))
    ]

    def sxcopy(k):
        return rcopy(sz.at[0], sz.at[(2, 1, 3)[k]], sxsend.at[k], sxrecv.at[k], at_x((1, 3, 2)[k]))

    def project():
        proj_copy.wait()
        scaled = (dot(pick_s[0], cot_ref[...]) * slotw_s[0]).astype(BF16)
        for e in range(EXPERTS):
            part = dot(scaled[e * PAD:(e + 1) * PAD], proj[e]).astype(BF16)
            for d in range(4):
                sps[d, e * PAD:(e + 1) * PAD, :] = part[:, d * 128:(d + 1) * 128]
        for cp in sycopies:
            cp.start()

    def project_send():
        for cp in sycopies:
            cp.wait_recv()
        total = sps[y].astype(F32)
        for k in range(3):
            total = total + spr[k].astype(F32)
        spz[...] = total.astype(BF16).reshape(EXPERTS, PAD, 128)
        for k in range(1, PIECES):
            zscopy(k).start()
        sz[0, 0] = spz[z // 2]

    def project_spread():
        for k in range(1, PIECES):
            zscopy(k).wait_recv()
        for k in range(3):
            sxcopy(k).start()

    for cp in weights:
        cp.wait()
    for cp in wwaits[:4]:
        cp.wait_recv()

    def ycopy(kind, i):
        src, dst, dev = {
            0: lambda: (p2.at[i, 0], ra.at[i], yr),
            1: lambda: (p2.at[i, 1], rb.at[i], yl),
            2: lambda: (pr.at[i, 1], fl.at[i, 1], yr),
            3: lambda: (pll.at[i, 0], fr.at[i, 0], yl),
            4: lambda: (pr.at[i, 0], fl.at[i, 0], yr),
            5: lambda: (pll.at[i, 1], fr.at[i, 1], yl),
            6: lambda: (hd.at[i, y], hd.at[i, y], yr),
            7: lambda: (hd.at[i, y], hd.at[i, y], yl),
            8: lambda: (hd.at[i, yl, 0], hd.at[i, yl, 0], yr),
            9: lambda: (hd.at[i, yr, 1], hd.at[i, yr, 1], yl),
        }[kind]()
        return rcopy(src, dst, ysend.at[kind, i], yrecv.at[kind, i], at_y(dev))

    def yarrive(kind, i):
        if kind < 6:
            ycopy(kind, i).wait_recv()
            return
        dst = {
            6: lambda: hd.at[i, yl],
            7: lambda: hd.at[i, yr],
            8: lambda: hd.at[i, yo, 0],
            9: lambda: hd.at[i, yo, 1],
        }[kind]()
        rcopy(dst, dst, ysend.at[kind, i], yrecv.at[kind, i], at_y(yr)).wait_recv()

    def stage0(i):
        for r in range(1, 4):
            xcopy(i, r).wait_recv()
        chunks = []
        for q in range(3):
            parts = []
            for r in range(4):
                parts += [xz[i, r, q * MAIN:(q + 1) * MAIN, :], xz[i, r, 3 * MAIN:, :]]
            chunks.append(dot(squeeze[q], jnp.concatenate(parts, axis=0)).astype(BF16))
        v = jnp.concatenate(chunks, axis=1)
        p2[i, 0] = dot(v, wg[yo]).astype(BF16)
        ycopy(0, i).start()
        p2[i, 1] = dot(v, wu[yo]).astype(BF16)
        ycopy(1, i).start()
        pr[i, 1] = dot(v, wu[yr]).astype(BF16)
        ycopy(2, i).start()
        pll[i, 0] = dot(v, wg[yl]).astype(BF16)
        ycopy(3, i).start()
        qa[i, 0] = dot(v, wg[yr])
        qa[i, 1] = dot(v, wu[yl])
        po[i, 0] = dot(v, wg[y])
        po[i, 1] = dot(v, wu[y])

    def stage1(i):
        yarrive(0, i)
        pr[i, 0] = (qa[i, 0] + ra[i].astype(F32)).astype(BF16)
        ycopy(4, i).start()
        yarrive(1, i)
        pll[i, 1] = (qa[i, 1] + rb[i].astype(F32)).astype(BF16)
        ycopy(5, i).start()

    def stage2(i):
        for kind in (2, 3, 4, 5):
            yarrive(kind, i)
        g = po[i, 0] + fl[i, 0].astype(F32) + fr[i, 0].astype(F32)
        u = po[i, 1] + fl[i, 1].astype(F32) + fr[i, 1].astype(F32)
        hidden = (g / (1.0 + jnp.exp(-g)) * u).astype(BF16)
        hd[i, y, 0] = hidden[:, :128]
        hd[i, y, 1] = hidden[:, 128:]
        ycopy(6, i).start()
        ycopy(7, i).start()

    def stage3(i):
        yarrive(6, i)
        ycopy(8, i).start()
        yarrive(7, i)
        ycopy(9, i).start()

    def ccopy(i, r):
        slot = {1: 2, 2: 1, 3: 3}[r]
        return rcopy(ob.at[i, r], cb.at[i, slot], csend.at[slot, i], crecv.at[slot, i], at_x({1: 1, 2: 3, 3: 2}[r]))

    def stage4(i):
        yarrive(8, i)
        yarrive(9, i)
        hidden = jnp.concatenate([hd[i, d, k] for d in range(4) for k in range(2)], axis=1)
        part = dot(hidden, wd[...].reshape(1024, 768)).astype(BF16)
        tail = 0.0
        for q in range(3):
            wide = dot(widen[q], part[:, q * 256:(q + 1) * 256]).reshape(4, PAD, 256)
            ob[i, :, q * MAIN:(q + 1) * MAIN, :] = wide[:, :MAIN].astype(BF16)
            tail = tail + wide[:, MAIN:]
        ob[i, :, 3 * MAIN:, :] = tail.astype(BF16)
        for r in range(1, 4):
            ccopy(i, r).start()
        rows = dot(squeeze[0], jnp.concatenate([sz[r, i] for r in range(4)], axis=0)).astype(BF16)
        lowt[...] += dot_t(rows, hidden)

    def rcopy_back(k):
        return rcopy(eb.at[k], rbk.at[z % 2, z // 2], rsend.at[k], rrecv.at[k], at_z(plane(k, 1)))

    def rarrive(k):
        come = plane(k, -1)
        dst = rbk.at[come % 2, come // 2]
        return rcopy(dst, dst, rsend.at[k], rrecv.at[k], at_z((z + 1) % 8))

    def stage5(i):
        for r in range(1, 4):
            ccopy(i, r).wait_recv()
        total = ob[i, 0].astype(F32)
        for r in range(1, 4):
            total = total + cb[i, r].astype(F32)
        eb[i] = total.astype(BF16)

        @pl.when(i > 0)
        def _():
            rcopy_back(i).start()

        @pl.when(i == 0)
        def _():
            rbk[z % 2, z // 2] = eb[0]

    def step(it, carry):
        def run(stage, lag):
            @pl.when((it >= lag) & (it < lag + PIECES))
            def _():
                stage(it - lag)

        run(stage3, LAG3)
        run(stage2, LAG2)
        run(stage1, LAG1)
        run(stage0, 0)

        @pl.when(it + 1 < PIECES)
        def _():
            zcopy(it + 1).wait_recv()
            spread(it + 1)

        @pl.when(it == 0)
        def _():
            project()

        @pl.when(it == 1)
        def _():
            project_send()

        @pl.when(it == 3)
        def _():
            project_spread()

        @pl.when(it == LAG4)
        def _():
            for k in range(3):
                sxcopy(k).wait_recv()
            down_copy.wait()
            wwaits[4].wait_recv()

        run(stage4, LAG4)
        run(stage5, LAG5)
        return carry

    lax.fori_loop(0, PIECES + LAG4, step, 0)

    lc[...] = lowt[...].T.reshape(2, 512, 128)
    lcc = rcopy(lc.at[1 - c], lr, lcsend, lcrecv, sibling)
    lcc.start()
    for i in range(PIECES + LAG4 - LAG5, PIECES):
        stage5(i)
    lcc.wait_recv()
    lo[y] = (lc[c] + lr[...]).astype(BF16)
    locopies = [rcopy(lo.at[y], lo.at[y], losend.at[k], lorecv.at[k], at_y(d)) for k, d in enumerate((yr, yl, yo))]
    lowaits = [rcopy(lo.at[d], lo.at[d], losend.at[k], lorecv.at[k], at_y(yr)) for k, d in enumerate((yl, yr, yo))]
    for cp in locopies:
        cp.start()
    for cp in lowaits:
        cp.wait_recv()
    low_ref[...] = lo[...]
    for k in range(1, PIECES):
        rarrive(k).wait_recv()
    for q in range(3):
        parts = []
        for e in range(EXPERTS):
            for part in (slice(q * MAIN, (q + 1) * MAIN), slice(3 * MAIN, BLOCK)):
                parts.append(rbk[0, e, part, :].astype(F32) + rbk[1, e, part, :].astype(F32))
        back = jnp.concatenate(parts, axis=0) * slotw_s[q]
        high = back.astype(BF16)
        rest = (back - high.astype(F32)).astype(BF16)
        mixed_ref[:, q * 256:(q + 1) * 256] = (dot_t(pick_s[q], high) + dot_t(pick_s[q], rest)).astype(BF16)

    for cp in wcopies + sycopies + locopies + [lcc]:
        cp.wait_send()
    for k in range(3):
        sxcopy(k).wait_send()

    def drain(i, carry):
        for kind in range(10):
            ycopy(kind, i).wait_send()
        for r in range(1, 4):
            ccopy(i, r).wait_send()
            xcopy(i, r).wait_send()

        @pl.when(i > 0)
        def _():
            zcopy(i).wait_send()
            zscopy(i).wait_send()
            rcopy_back(i).wait_send()

        return carry

    lax.fori_loop(0, PIECES, drain, 0)


def moe(ids, route, tokens, cotangent, gate, up, down, projector):
    vm = lambda *shape: pltpu.VMEM(shape, BF16)
    vf = lambda *shape: pltpu.VMEM(shape, F32)
    sem = lambda *shape: pltpu.SemaphoreType.DMA(shape)
    n = PIECES
    scratch = [
        pltpu.VMEM((2, 64), jnp.int32), vf(2, 64), vm(64, 768), vm(64, 768),
        vm(4, 768, 256), vm(4, 768, 256), vm(2, 512, 768), vm(4, 768, 512),
        vm(3, 192, 64), vf(3, 192, 1), vm(3, ROWS, 192), vm(3, 192, ROWS),
        vm(4, BLOCK, 256), vm(n, 4, BLOCK, 256), vm(4, 192, 128), vm(3, 192, 128), vm(4, PAD, 128), vm(4, n, PAD, 128),
        vm(n, 2, ROWS, 256), vm(n, 2, ROWS, 256), vm(n, 2, ROWS, 256), vf(n, 2, ROWS, 256), vf(n, 2, ROWS, 256),
        vm(n, ROWS, 256), vm(n, ROWS, 256), vm(n, 2, ROWS, 256), vm(n, 2, ROWS, 256),
        vm(n, 4, 2, ROWS, 128), vm(n, 4, BLOCK, 256), vm(n, 4, BLOCK, 256), vm(n, BLOCK, 256), vm(2, 4, BLOCK, 256),
        vf(128, 1024), vf(2, 512, 128), vf(512, 128), vm(4, 512, 128),
        sem(10), sem(5), sem(5), sem(n), sem(n), sem(n), sem(n), sem(3), sem(3), sem(3), sem(3),
        sem(4, n), sem(4, n), sem(10, n), sem(10, n), sem(4, n), sem(4, n), sem(n), sem(n),
        pltpu.SemaphoreType.DMA, pltpu.SemaphoreType.DMA, sem(3), sem(3),
    ]
    vmem = pl.BlockSpec(memory_space=pltpu.VMEM)
    hbm = pl.BlockSpec(memory_space=pl.ANY)
    return pl.pallas_call(
        moe_kernel,
        out_shape=(
            jax.ShapeDtypeStruct((64, 768), BF16),
            jax.ShapeDtypeStruct((4, 512, 128), BF16),
        ),
        in_specs=[hbm] * 8,
        out_specs=(vmem, vmem),
        scratch_shapes=scratch,
        compiler_params=pltpu.CompilerParams(
            collective_id=0, has_side_effects=True, vmem_limit_bytes=52 * 1024 * 1024
        ),
        cost_estimate=pl.CostEstimate(flops=8_000_000_000, bytes_accessed=6_000_000, transcendentals=300_000),
        name="moe",
    )(ids, route, tokens, cotangent, gate, up, down, projector)


def update_kernel(expert_ref, low_ref, first_ref, second_ref, proj_ref, update_ref, new_first_ref, new_second_ref):
    low = jnp.concatenate([low_ref[d] for d in range(4)], axis=1).astype(F32)
    new_first = 0.9 * first_ref[...] + 0.1 * low
    new_second = 0.999 * second_ref[...] + 0.001 * low * low
    new_first_ref[...] = new_first
    new_second_ref[...] = new_second
    bias_one = 1.0 - 0.9**10
    bias_two = 1.0 - 0.999**10
    direction = new_first / bias_one / (jnp.sqrt(new_second / bias_two) + 1e-08)
    high = direction.astype(BF16)
    rest = (direction - high.astype(F32)).astype(BF16)
    basis = proj_ref[0]
    dims = (((1,), (1,)), ((), ()))
    update_ref[...] = lax.dot_general(high, basis, dims, preferred_element_type=F32) + lax.dot_general(
        rest, basis, dims, preferred_element_type=F32
    )


def update_step(expert, low, first, second, projector):
    rows = 128
    return pl.pallas_call(
        update_kernel,
        out_shape=(
            jax.ShapeDtypeStruct((512, 768), F32),
            jax.ShapeDtypeStruct((512, 512), F32),
            jax.ShapeDtypeStruct((512, 512), F32),
        ),
        grid_spec=pltpu.PrefetchScalarGridSpec(
            num_scalar_prefetch=1,
            grid=(512 // rows,),
            in_specs=[
                pl.BlockSpec((4, rows, 128), lambda i, e: (0, i, 0)),
                pl.BlockSpec((rows, 512), lambda i, e: (i, 0)),
                pl.BlockSpec((rows, 512), lambda i, e: (i, 0)),
                pl.BlockSpec((1, 768, 512), lambda i, e: (e[0], 0, 0)),
            ],
            out_specs=(
                pl.BlockSpec((rows, 768), lambda i, e: (i, 0)),
                pl.BlockSpec((rows, 512), lambda i, e: (i, 0)),
                pl.BlockSpec((rows, 512), lambda i, e: (i, 0)),
            ),
        ),
        cost_estimate=pl.CostEstimate(flops=800_000_000, bytes_accessed=7_000_000, transcendentals=300_000),
        name="update",
    )(expert, low, first, second, projector)


def body(
    tokens,
    cotangent,
    expert_ids,
    route_weights,
    gate_weight,
    up_weight,
    down_weight,
    projector,
    first_moment,
    second_moment,
):
    mixed, low = moe(
        expert_ids.T, route_weights.T, tokens, cotangent, gate_weight, up_weight, down_weight, projector
    )
    expert = (lax.axis_index("fsdp") // 16).astype(jnp.int32).reshape(1)
    update, new_first, new_second = update_step(expert, low, first_moment, second_moment, projector)
    return mixed, update, new_first, new_second


def solution(mesh):
    in_specs = (
        P("fsdp", "tp"),
        P("fsdp", "tp"),
        P("fsdp", None),
        P("fsdp", None),
        P("tp", "fsdp"),
        P("tp", "fsdp"),
        P("fsdp", "tp"),
        P(None, "tp", None),
        P("fsdp", None),
        P("fsdp", None),
    )
    out_specs = (P("fsdp", "tp"), P("fsdp", "tp"), P("fsdp", None), P("fsdp", None))
    return jax.shard_map(body, mesh=mesh, in_specs=in_specs, out_specs=out_specs, check_vma=False)
```

time: 113 us -> 110 us (0.973)
  Pallas kernels: 105 us -> 102 us
    pallas_call x1, Pallas kernels: 98.9 us -> 96.5 us  [moe(): pl.pallas_call(moe_kernel, out_shape=(jax.ShapeDtypeStruct((64, 768), BF1...]
where the time goes in v2:
time: 110 us; the launch traced here: 108 us
  Pallas kernels  102 us (93%)
  local copies, waits for them, and re-layouts  5.69 us (5%)
    pallas_call x1, Pallas kernels, moe(): pl.pallas_call(moe_kernel, out_shape=(jax.ShapeDtypeStruct((64, 768), BF1...  96.5 us
    unnamed x13, local copies, waits for them, and re-layouts  5.69 us
    pallas_call x1, Pallas kernels, update_step(): pl.pallas_call(update_kernel, out_shape=(jax.ShapeDtypeStruct((512, 768),...  5.58 us

profile of v2, /device:TPU:8, one launch (start us, length us, event | category | flops | bytes accessed | tf_op | source)
XLA Modules:
  0.0 108.4 jit_solution(13184206220869478097)
XLA Ops:
  0.6 0.0 copy-start.1
  0.7 1.1 %copy-done.1 = bf16[768,512]{1,0:T(8,128)(2,1)S(1)} copy-done((bf16[768,512]{1,0:T(8,128)(2,1)S(1)}, bf16[768,512]{1,0:T(8,128)(2,1)}, u32[]{:S(2)}) %copy-start.1) | copy-done | bytes 786456
  1.8 0.0 copy-start.2
  1.8 0.9 copy-done.2
  2.7 0.0 copy-start.3
  2.7 0.9 copy-done.3
  3.6 0.0 copy-start.4
  3.6 0.7 copy-done.4
  4.2 0.0 copy-start.5
  4.3 0.7 copy-done.5
  4.9 96.5 %moe.1 = (bf16[64,768]{1,0:T(8,128)(2,1)S(1)}, bf16[4,512,128]{2,1,0:T(8,128)(2,1)S(1)}) custom-call(s32[2,64]{1,0:T(2,128)S(1)} %bitcast.3, f32[2,64]{1,0:T(2,128)S(1)} %bitcast.4, bf16[64,768]{1,0:T(8,128)(2,1)S(1)} %copy-done.2, bf16[64,768]{1,0:T(8,128)(2,1)S(1)} %copy-done.3, bf16[768,512]{1,0:T(8,128)(2,1)S(1)} %copy-done.1, bf16[768,512]{1,0:T(8,128)(2,1)} %wu_hbm.1, ...), custom_call_target="tpu_custom_call" | custom-call | flops 8000000000 | bytes 6000000 | tf_op jit(solution)/shard_map/moe/pallas_call | solution.py:428
  101.4 0.0 copy-start
  101.4 0.8 copy-done
  102.2 5.6 %update.1 = (f32[512,768]{1,0:T(8,128)}, f32[512,512]{1,0:T(8,128)}, f32[512,512]{1,0:T(8,128)}) custom-call(s32[1]{0:T(128)} %bitcast.2.expert_ref, bf16[4,512,128]{2,1,0:T(8,128)(2,1)} %copy-done, f32[512,512]{1,0:T(8,128)} %first_ref.1, f32[512,512]{1,0:T(8,128)} %second_ref.1, bf16[4,768,512]{2,1,0:T(8,128)(2,1)} %proj_ref.1), custom_call_target="tpu_custom_call" | custom-call | flops 800000000 | bytes 7000000 | tf_op jit(solution)/shard_map/update/pallas_call | solution.py:465
  107.8 0.6 copy.15
Async XLA Ops:
  0.6 1.1 %copy-start.1 = (bf16[768,512]{1,0:T(8,128)(2,1)S(1)}, bf16[768,512]{1,0:T(8,128)(2,1)}, u32[]{:S(2)}) copy-start(bf16[768,512]{1,0:T(8,128)(2,1)} %wg_hbm.1) | copy-start | bytes 2359300
  1.8 0.9 copy-start.2
  2.7 0.9 copy-start.3
  3.6 0.7 copy-start.4
  4.2 0.7 copy-start.5
  101.4 0.8 copy-start

commit v3 on v2

--- a/solution.py
+++ b/solution.py
@@ -8,10 +8,11 @@
 EXPERTS = 4
 MOST = 36
 MAIN, REST, BLOCK = 32, 16, 112
+SLIM = 2 * MAIN + REST
 PAD = MAIN + REST
 ROWS = 4 * MOST
 PIECES = 8
-RELZ = (0, 1, 2, 3, 4, -3, -2, -1)
+RELZ = (0, 1, 2, -2, 3, -3, 4, -1)
 LAG1, LAG2, LAG3, LAG4, LAG5 = 1, 2, 3, 4, 5
 MESH = pl.DeviceIdType.MESH
 F32, BF16 = jnp.float32, jnp.bfloat16
@@ -46,9 +47,9 @@
     mixed_ref, low_ref,
     ids_ref, route_ref, tok_ref, cot_ref,
     wg, wu, wd, proj, pick_s, slotw_s, squeeze, widen, xs, xz, sps, spr, spz, sz,
-    p2, pr, pll, qa, po, ra, rb, fl, fr, hd, ob, cb, eb, rbk, lowt, lc, lr, lo,
-    lsem, wsend, wrecv, zsend, zrecv, zssend, zsrecv, sysend, syrecv, sxsend, sxrecv,
-    xsend, xrecv, ysend, yrecv, csend, crecv, rsend, rrecv, lcsend, lcrecv, losend, lorecv,
+    p2, pr, pll, qa, po, ra, rb, fl, fr, hd, ob, cb, eb, rbk, lowa, lc, lr,
+    lsem, wsend, wrecv, zsend, zrecv, zssend, zsrecv, sysend, syrecv, sgsend, sgrecv, sxsend, sxrecv,
+    xsend, xrecv, ysend, yrecv, csend, crecv, rsend, rrecv, lcsend, lcrecv,
 ):
     f = lax.axis_index("fsdp")
     y = lax.axis_index("tp")
@@ -65,7 +66,11 @@
         return (zz * 8 + x * 2 + c, y)
 
     def plane(k, sign):
-        rel = jnp.where(k < 5, k, k - 8)
+        if isinstance(k, int):
+            return (z + 8 + sign * RELZ[k]) % 8
+        rel = jnp.int32(RELZ[0])
+        for n in range(1, PIECES):
+            rel = jnp.where(k == n, RELZ[n], rel)
         return (z + 8 + sign * rel) % 8
 
     sibling = (z * 8 + x * 2 + (1 - c), y)
@@ -90,8 +95,8 @@
         cp.start()
 
     barrier = pltpu.get_barrier_semaphore()
-    partners = [at_y(yr), at_y(yl), at_y(yo), at_x(1), at_x(3), at_x(2), sibling]
-    partners += [at_z((z + k) % 8) for k in range(1, 8)]
+    partners = [at_z((z + k) % 8) for k in (4, 3, 5, 2, 6, 1, 7)]
+    partners += [at_y(yo), at_x(2), at_y(yr), at_y(yl), at_x(1), at_x(3), sibling]
     for dev in partners:
         pl.semaphore_signal(barrier, inc=1, device_id=dev, device_id_type=MESH)
 
@@ -119,6 +124,11 @@
         tail = tail + rows[:, MAIN:]
     xs[:, 3 * MAIN:, :] = tail.astype(BF16)
 
+    for q in range(3):
+        squeeze[q] = matcher((ROWS, 4 * PAD), 0, q)
+        widen[q] = matcher((4 * PAD, ROWS), 1, q)
+    lowa[...] = jnp.zeros_like(lowa)
+
     pl.semaphore_wait(barrier, len(partners))
 
     def zcopy(k):
@@ -148,11 +158,6 @@
     for cp in wcopies:
         cp.start()
 
-    for q in range(3):
-        squeeze[q] = matcher((ROWS, 4 * PAD), 0, q)
-        widen[q] = matcher((4 * PAD, ROWS), 1, q)
-    lowt[...] = jnp.zeros_like(lowt)
-
     def zscopy(k):
         there = plane(k, -1)
         return rcopy(spz.at[there // 2], sz.at[0, k], zssend.at[k], zsrecv.at[k], at_z(there))
@@ -160,37 +165,48 @@
     sycopies = [
         rcopy(sps.at[d], spr.at[k], sysend.at[k], syrecv.at[k], at_y(d)) for k, d in enumerate((yr, yl, yo))
     ]
-
-    def sxcopy(k):
-        return rcopy(sz.at[0], sz.at[(2, 1, 3)[k]], sxsend.at[k], sxrecv.at[k], at_x((1, 3, 2)[k]))
+    sgcopies = [
+        rcopy(spz.at[y], spz.at[y], sgsend.at[k], sgrecv.at[k], at_y(d)) for k, d in enumerate((yr, yl, yo))
+    ]
+    sgwaits = [
+        rcopy(spz.at[d], spz.at[d], sgsend.at[k], sgrecv.at[k], at_y(yr)) for k, d in enumerate((yl, yr, yo))
+    ]
+
+    def sxcopy(k, r):
+        return rcopy(sz.at[0, k], sz.at[r, k], sxsend.at[r, k], sxrecv.at[r, k], at_x({2: 1, 1: 3, 3: 2}[r]))
 
     def project():
         proj_copy.wait()
-        scaled = (dot(pick_s[0], cot_ref[...]) * slotw_s[0]).astype(BF16)
+        tails = [0.0] * EXPERTS
+        for q in range(2):
+            scaled = (dot(pick_s[q], cot_ref[...]) * slotw_s[q]).astype(BF16)
+            for e in range(EXPERTS):
+                part = dot(scaled[e * PAD:(e + 1) * PAD], proj[e, :, q * 256:(q + 1) * 256])
+                sps[e, q * MAIN:(q + 1) * MAIN, :] = part[:MAIN].astype(BF16)
+                tails[e] = tails[e] + part[MAIN:]
         for e in range(EXPERTS):
-            part = dot(scaled[e * PAD:(e + 1) * PAD], proj[e]).astype(BF16)
-            for d in range(4):
-                sps[d, e * PAD:(e + 1) * PAD, :] = part[:, d * 128:(d + 1) * 128]
+            sps[e, 2 * MAIN:, :] = tails[e].astype(BF16)
         for cp in sycopies:
             cp.start()
 
-    def project_send():
+    def project_sum():
         for cp in sycopies:
             cp.wait_recv()
         total = sps[y].astype(F32)
         for k in range(3):
             total = total + spr[k].astype(F32)
-        spz[...] = total.astype(BF16).reshape(EXPERTS, PAD, 128)
+        spz[y] = total.astype(BF16)
+        for cp in sgcopies:
+            cp.start()
+
+    def project_send():
+        for cp in sgwaits:
+            cp.wait_recv()
         for k in range(1, PIECES):
             zscopy(k).start()
         sz[0, 0] = spz[z // 2]
 
-    def project_spread():
-        for k in range(1, PIECES):
-            zscopy(k).wait_recv()
-        for k in range(3):
-            sxcopy(k).start()
-
+    project()
     for cp in weights:
         cp.wait()
     for cp in wwaits[:4]:
@@ -275,10 +291,29 @@
         slot = {1: 2, 2: 1, 3: 3}[r]
         return rcopy(ob.at[i, r], cb.at[i, slot], csend.at[slot, i], crecv.at[slot, i], at_x({1: 1, 2: 3, 3: 2}[r]))
 
+    lcc = rcopy(lc, lr, lcsend, lcrecv, sibling)
+
     def stage4(i):
         yarrive(8, i)
         yarrive(9, i)
         hidden = jnp.concatenate([hd[i, d, k] for d in range(4) for k in range(2)], axis=1)
+        for r in range(1, 4):
+            sxcopy(i, r).wait_recv()
+        chunks = []
+        for q in range(2):
+            parts = []
+            for r in range(4):
+                parts += [sz[r, i, q * MAIN:(q + 1) * MAIN, :], sz[r, i, 2 * MAIN:, :]]
+            chunks.append(dot(squeeze[q], jnp.concatenate(parts, axis=0)).astype(BF16))
+        rows = jnp.concatenate(chunks, axis=1)
+        for k in range(2):
+            lowa[k] += dot_t(hidden[:, k * 512:(k + 1) * 512], rows)
+
+        @pl.when(i == PIECES - 1)
+        def _():
+            lc[...] = lowa[1 - c].astype(BF16)
+            lcc.start()
+
         part = dot(hidden, wd[...].reshape(1024, 768)).astype(BF16)
         tail = 0.0
         for q in range(3):
@@ -288,8 +323,6 @@
         ob[i, :, 3 * MAIN:, :] = tail.astype(BF16)
         for r in range(1, 4):
             ccopy(i, r).start()
-        rows = dot(squeeze[0], jnp.concatenate([sz[r, i] for r in range(4)], axis=0)).astype(BF16)
-        lowt[...] += dot_t(rows, hidden)
 
     def rcopy_back(k):
         return rcopy(eb.at[k], rbk.at[z % 2, z // 2], rsend.at[k], rrecv.at[k], at_z(plane(k, 1)))
@@ -333,20 +366,23 @@
 
         @pl.when(it == 0)
         def _():
-            project()
+            project_sum()
 
         @pl.when(it == 1)
         def _():
             project_send()
 
-        @pl.when(it == 3)
-        def _():
-            project_spread()
+        @pl.when((it >= 2) & (it < 2 + PIECES))
+        def _():
+            @pl.when(it > 2)
+            def _():
+                zscopy(it - 2).wait_recv()
+
+            for r in (2, 1, 3):
+                sxcopy(it - 2, r).start()
 
         @pl.when(it == LAG4)
         def _():
-            for k in range(3):
-                sxcopy(k).wait_recv()
             down_copy.wait()
             wwaits[4].wait_recv()
 
@@ -356,20 +392,10 @@
 
     lax.fori_loop(0, PIECES + LAG4, step, 0)
 
-    lc[...] = lowt[...].T.reshape(2, 512, 128)
-    lcc = rcopy(lc.at[1 - c], lr, lcsend, lcrecv, sibling)
-    lcc.start()
     for i in range(PIECES + LAG4 - LAG5, PIECES):
         stage5(i)
     lcc.wait_recv()
-    lo[y] = (lc[c] + lr[...]).astype(BF16)
-    locopies = [rcopy(lo.at[y], lo.at[y], losend.at[k], lorecv.at[k], at_y(d)) for k, d in enumerate((yr, yl, yo))]
-    lowaits = [rcopy(lo.at[d], lo.at[d], losend.at[k], lorecv.at[k], at_y(yr)) for k, d in enumerate((yl, yr, yo))]
-    for cp in locopies:
-        cp.start()
-    for cp in lowaits:
-        cp.wait_recv()
-    low_ref[...] = lo[...]
+    low_ref[...] = (lowa[c] + lr[...].astype(F32)).astype(BF16)
     for k in range(1, PIECES):
         rarrive(k).wait_recv()
     for q in range(3):
@@ -382,10 +408,8 @@
         rest = (back - high.astype(F32)).astype(BF16)
         mixed_ref[:, q * 256:(q + 1) * 256] = (dot_t(pick_s[q], high) + dot_t(pick_s[q], rest)).astype(BF16)
 
-    for cp in wcopies + sycopies + locopies + [lcc]:
+    for cp in wcopies + sycopies + sgcopies + [lcc]:
         cp.wait_send()
-    for k in range(3):
-        sxcopy(k).wait_send()
 
     def drain(i, carry):
         for kind in range(10):
@@ -393,6 +417,7 @@
         for r in range(1, 4):
             ccopy(i, r).wait_send()
             xcopy(i, r).wait_send()
+            sxcopy(i, r).wait_send()
 
         @pl.when(i > 0)
         def _():
@@ -414,14 +439,14 @@
         pltpu.VMEM((2, 64), jnp.int32), vf(2, 64), vm(64, 768), vm(64, 768),
         vm(4, 768, 256), vm(4, 768, 256), vm(2, 512, 768), vm(4, 768, 512),
         vm(3, 192, 64), vf(3, 192, 1), vm(3, ROWS, 192), vm(3, 192, ROWS),
-        vm(4, BLOCK, 256), vm(n, 4, BLOCK, 256), vm(4, 192, 128), vm(3, 192, 128), vm(4, PAD, 128), vm(4, n, PAD, 128),
+        vm(4, BLOCK, 256), vm(n, 4, BLOCK, 256), vm(4, SLIM, 256), vm(3, SLIM, 256), vm(4, SLIM, 256), vm(4, n, SLIM, 256),
         vm(n, 2, ROWS, 256), vm(n, 2, ROWS, 256), vm(n, 2, ROWS, 256), vf(n, 2, ROWS, 256), vf(n, 2, ROWS, 256),
         vm(n, ROWS, 256), vm(n, ROWS, 256), vm(n, 2, ROWS, 256), vm(n, 2, ROWS, 256),
         vm(n, 4, 2, ROWS, 128), vm(n, 4, BLOCK, 256), vm(n, 4, BLOCK, 256), vm(n, BLOCK, 256), vm(2, 4, BLOCK, 256),
-        vf(128, 1024), vf(2, 512, 128), vf(512, 128), vm(4, 512, 128),
-        sem(10), sem(5), sem(5), sem(n), sem(n), sem(n), sem(n), sem(3), sem(3), sem(3), sem(3),
+        vf(2, 512, 512), vm(512, 512), vm(512, 512),
+        sem(10), sem(5), sem(5), sem(n), sem(n), sem(n), sem(n), sem(3), sem(3), sem(3), sem(3), sem(4, n), sem(4, n),
         sem(4, n), sem(4, n), sem(10, n), sem(10, n), sem(4, n), sem(4, n), sem(n), sem(n),
-        pltpu.SemaphoreType.DMA, pltpu.SemaphoreType.DMA, sem(3), sem(3),
+        pltpu.SemaphoreType.DMA, pltpu.SemaphoreType.DMA,
     ]
     vmem = pl.BlockSpec(memory_space=pltpu.VMEM)
     hbm = pl.BlockSpec(memory_space=pl.ANY)
@@ -429,21 +454,24 @@
         moe_kernel,
         out_shape=(
             jax.ShapeDtypeStruct((64, 768), BF16),
-            jax.ShapeDtypeStruct((4, 512, 128), BF16),
+            jax.ShapeDtypeStruct((512, 512), BF16),
         ),
         in_specs=[hbm] * 8,
         out_specs=(vmem, vmem),
         scratch_shapes=scratch,
         compiler_params=pltpu.CompilerParams(
-            collective_id=0, has_side_effects=True, vmem_limit_bytes=52 * 1024 * 1024
+            collective_id=0, has_side_effects=True, vmem_limit_bytes=65000 * 1024
         ),
         cost_estimate=pl.CostEstimate(flops=8_000_000_000, bytes_accessed=6_000_000, transcendentals=300_000),
         name="moe",
     )(ids, route, tokens, cotangent, gate, up, down, projector)
 
 
-def update_kernel(expert_ref, low_ref, first_ref, second_ref, proj_ref, update_ref, new_first_ref, new_second_ref):
-    low = jnp.concatenate([low_ref[d] for d in range(4)], axis=1).astype(F32)
+def update_kernel(
+    expert_ref, low_ref, first_ref, second_ref, proj_ref, mixed_ref, update_ref, new_first_ref, new_second_ref, out_ref
+):
+    out_ref[...] = mixed_ref[...]
+    low = low_ref[...].astype(F32)
     new_first = 0.9 * first_ref[...] + 0.1 * low
     new_second = 0.999 * second_ref[...] + 0.001 * low * low
     new_first_ref[...] = new_first
@@ -460,33 +488,36 @@
     )
 
 
-def update_step(expert, low, first, second, projector):
-    rows = 128
+def update_step(expert, low, first, second, projector, mixed):
+    rows = 256
     return pl.pallas_call(
         update_kernel,
         out_shape=(
             jax.ShapeDtypeStruct((512, 768), F32),
             jax.ShapeDtypeStruct((512, 512), F32),
             jax.ShapeDtypeStruct((512, 512), F32),
+            jax.ShapeDtypeStruct((64, 768), BF16),
         ),
         grid_spec=pltpu.PrefetchScalarGridSpec(
             num_scalar_prefetch=1,
             grid=(512 // rows,),
             in_specs=[
-                pl.BlockSpec((4, rows, 128), lambda i, e: (0, i, 0)),
+                pl.BlockSpec((rows, 512), lambda i, e: (i, 0)),
                 pl.BlockSpec((rows, 512), lambda i, e: (i, 0)),
                 pl.BlockSpec((rows, 512), lambda i, e: (i, 0)),
                 pl.BlockSpec((1, 768, 512), lambda i, e: (e[0], 0, 0)),
+                pl.BlockSpec((rows // 8, 768), lambda i, e: (i, 0)),
             ],
             out_specs=(
                 pl.BlockSpec((rows, 768), lambda i, e: (i, 0)),
                 pl.BlockSpec((rows, 512), lambda i, e: (i, 0)),
                 pl.BlockSpec((rows, 512), lambda i, e: (i, 0)),
+                pl.BlockSpec((rows // 8, 768), lambda i, e: (i, 0)),
             ),
         ),
         cost_estimate=pl.CostEstimate(flops=800_000_000, bytes_accessed=7_000_000, transcendentals=300_000),
         name="update",
-    )(expert, low, first, second, projector)
+    )(expert, low, first, second, projector, mixed)
 
 
 def body(
@@ -505,7 +536,9 @@
         expert_ids.T, route_weights.T, tokens, cotangent, gate_weight, up_weight, down_weight, projector
     )
     expert = (lax.axis_index("fsdp") // 16).astype(jnp.int32).reshape(1)
-    update, new_first, new_second = update_step(expert, low, first_moment, second_moment, projector)
+    update, new_first, new_second, mixed = update_step(
+        expert, low, first_moment, second_moment, projector, mixed
+    )
     return mixed, update, new_first, new_second
 
 

time: 110 us -> 99.2 us (0.902); the launches traced: 108 us -> 99.1 us
  local copies, waits for them, and re-layouts: 5.69 us -> 0 us
  Pallas kernels: 102 us -> 98.5 us
    unnamed x13 -> x0, local copies, waits for them, and re-layouts: 5.69 us -> none
    pallas_call x1, Pallas kernels: 96.5 us -> 94.1 us  [moe(): pl.pallas_call(moe_kernel, out_shape=(jax.ShapeDtypeStruct((64, 768), BF1...]
    pallas_call x1, Pallas kernels: 5.58 us -> 4.42 us  [update_step(): pl.pallas_call(update_kernel, out_shape=(jax.ShapeDtypeStruct((512, 768),...]
where the time goes in v3:
time: 99.2 us; the launch traced here: 99.1 us
  Pallas kernels  98.5 us (99%)
    pallas_call x1, Pallas kernels, moe(): pl.pallas_call(moe_kernel, out_shape=(jax.ShapeDtypeStruct((64, 768), BF1...  94.1 us
    pallas_call x1, Pallas kernels, update_step(): pl.pallas_call(update_kernel, out_shape=(jax.ShapeDtypeStruct((512, 768),...  4.42 us

profile of v3, /device:TPU:8, one launch (start us, length us, event | category | flops | bytes accessed | tf_op | source)
XLA Modules:
  0.0 99.1 jit_solution(15611242683173852956)
XLA Ops:
  0.6 94.1 %moe.1 = (bf16[64,768]{1,0:T(8,128)(2,1)}, bf16[512,512]{1,0:T(8,128)(2,1)}) custom-call(s32[2,64]{1,0:T(2,128)} %bitcast.3, f32[2,64]{1,0:T(2,128)} %bitcast.4, bf16[64,768]{1,0:T(8,128)(2,1)} %tok_hbm.1, bf16[64,768]{1,0:T(8,128)(2,1)} %cot_hbm.1, bf16[768,512]{1,0:T(8,128)(2,1)} %wg_hbm.1, bf16[768,512]{1,0:T(8,128)(2,1)} %wu_hbm.1, ...), custom_call_target="tpu_custom_call" | custom-call | flops 8000000000 | bytes 6000000 | tf_op jit(solution)/shard_map/moe/pallas_call | solution.py:453
  94.7 4.4 %update.1 = (f32[512,768]{1,0:T(8,128)}, f32[512,512]{1,0:T(8,128)}, f32[512,512]{1,0:T(8,128)}, bf16[64,768]{1,0:T(8,128)(2,1)}) custom-call(s32[1]{0:T(128)} %bitcast.expert_ref, bf16[512,512]{1,0:T(8,128)(2,1)} %get-tuple-element.10.low_ref, f32[512,512]{1,0:T(8,128)} %first_ref.1, f32[512,512]{1,0:T(8,128)} %second_ref.1, bf16[4,768,512]{2,1,0:T(8,128)(2,1)} %proj_ref.1, ...), custom_call_target="tpu_custom_call" | custom-call | flops 800000000 | bytes 7000000 | tf_op jit(solution)/shard_map/update/pallas_call | solution.py:493

commit v4 on v3

--- a/solution.py
+++ b/solution.py
@@ -129,6 +129,17 @@
         widen[q] = matcher((4 * PAD, ROWS), 1, q)
     lowa[...] = jnp.zeros_like(lowa)
 
+    proj_copy.wait()
+    tails = [0.0] * EXPERTS
+    for q in range(2):
+        scaled = (dot(pick_s[q], cot_ref[...]) * slotw_s[q]).astype(BF16)
+        for e in range(EXPERTS):
+            part = dot(scaled[e * PAD:(e + 1) * PAD], proj[e, :, q * 256:(q + 1) * 256])
+            sps[e, q * MAIN:(q + 1) * MAIN, :] = part[:MAIN].astype(BF16)
+            tails[e] = tails[e] + part[MAIN:]
+    for e in range(EXPERTS):
+        sps[e, 2 * MAIN:, :] = tails[e].astype(BF16)
+
     pl.semaphore_wait(barrier, len(partners))
 
     def zcopy(k):
@@ -144,8 +155,6 @@
 
     xz[0, 0] = xs[z // 2]
     spread(0)
-    for k in range(1, PIECES):
-        zcopy(k).start()
 
     remote = []
     for k in range(2):
@@ -157,6 +166,8 @@
     wwaits = [rcopy(s, d.at[theirs], wsend.at[n], wrecv.at[n], sibling) for n, (s, d, _, theirs) in enumerate(remote)]
     for cp in wcopies:
         cp.start()
+    for k in range(1, PIECES):
+        zcopy(k).start()
 
     def zscopy(k):
         there = plane(k, -1)
@@ -172,22 +183,11 @@
         rcopy(spz.at[d], spz.at[d], sgsend.at[k], sgrecv.at[k], at_y(yr)) for k, d in enumerate((yl, yr, yo))
     ]
 
+    for cp in sycopies:
+        cp.start()
+
     def sxcopy(k, r):
         return rcopy(sz.at[0, k], sz.at[r, k], sxsend.at[r, k], sxrecv.at[r, k], at_x({2: 1, 1: 3, 3: 2}[r]))
-
-    def project():
-        proj_copy.wait()
-        tails = [0.0] * EXPERTS
-        for q in range(2):
-            scaled = (dot(pick_s[q], cot_ref[...]) * slotw_s[q]).astype(BF16)
-            for e in range(EXPERTS):
-                part = dot(scaled[e * PAD:(e + 1) * PAD], proj[e, :, q * 256:(q + 1) * 256])
-                sps[e, q * MAIN:(q + 1) * MAIN, :] = part[:MAIN].astype(BF16)
-                tails[e] = tails[e] + part[MAIN:]
-        for e in range(EXPERTS):
-            sps[e, 2 * MAIN:, :] = tails[e].astype(BF16)
-        for cp in sycopies:
-            cp.start()
 
     def project_sum():
         for cp in sycopies:
@@ -206,7 +206,7 @@
             zscopy(k).start()
         sz[0, 0] = spz[z // 2]
 
-    project()
+    project_sum()
     for cp in weights:
         cp.wait()
     for cp in wwaits[:4]:
@@ -254,13 +254,13 @@
         p2[i, 1] = dot(v, wu[yo]).astype(BF16)
         ycopy(1, i).start()
         pr[i, 1] = dot(v, wu[yr]).astype(BF16)
-        ycopy(2, i).start()
         pll[i, 0] = dot(v, wg[yl]).astype(BF16)
-        ycopy(3, i).start()
         qa[i, 0] = dot(v, wg[yr])
         qa[i, 1] = dot(v, wu[yl])
         po[i, 0] = dot(v, wg[y])
         po[i, 1] = dot(v, wu[y])
+        ycopy(3, i).start()
+        ycopy(2, i).start()
 
     def stage1(i):
         yarrive(0, i)
@@ -297,6 +297,16 @@
         yarrive(8, i)
         yarrive(9, i)
         hidden = jnp.concatenate([hd[i, d, k] for d in range(4) for k in range(2)], axis=1)
+        part = dot(hidden, wd[...].reshape(1024, 768)).astype(BF16)
+        tail = 0.0
+        for q in range(3):
+            wide = dot(widen[q], part[:, q * 256:(q + 1) * 256]).reshape(4, PAD, 256)
+            ob[i, :, q * MAIN:(q + 1) * MAIN, :] = wide[:, :MAIN].astype(BF16)
+            tail = tail + wide[:, MAIN:]
+        ob[i, :, 3 * MAIN:, :] = tail.astype(BF16)
+        for r in range(1, 4):
+            ccopy(i, r).start()
+
         for r in range(1, 4):
             sxcopy(i, r).wait_recv()
         chunks = []
@@ -314,16 +324,6 @@
             lc[...] = lowa[1 - c].astype(BF16)
             lcc.start()
 
-        part = dot(hidden, wd[...].reshape(1024, 768)).astype(BF16)
-        tail = 0.0
-        for q in range(3):
-            wide = dot(widen[q], part[:, q * 256:(q + 1) * 256]).reshape(4, PAD, 256)
-            ob[i, :, q * MAIN:(q + 1) * MAIN, :] = wide[:, :MAIN].astype(BF16)
-            tail = tail + wide[:, MAIN:]
-        ob[i, :, 3 * MAIN:, :] = tail.astype(BF16)
-        for r in range(1, 4):
-            ccopy(i, r).start()
-
     def rcopy_back(k):
         return rcopy(eb.at[k], rbk.at[z % 2, z // 2], rsend.at[k], rrecv.at[k], at_z(plane(k, 1)))
 
@@ -332,7 +332,27 @@
         dst = rbk.at[come % 2, come // 2]
         return rcopy(dst, dst, rsend.at[k], rrecv.at[k], at_z((z + 1) % 8))
 
+    def returned(i):
+        for r in range(1, 4):
+            ccopy(i, r).wait_send()
+
+        @pl.when(i > 0)
+        def _():
+            rcopy_back(i).wait_send()
+
     def stage5(i):
+        for kind in range(10):
+            ycopy(kind, i).wait_send()
+        for r in range(1, 4):
+            xcopy(i, r).wait_send()
+            sxcopy(i, r).wait_send()
+
+        @pl.when(i > 0)
+        def _():
+            zcopy(i).wait_send()
+            zscopy(i).wait_send()
+            returned(i - 1)
+
         for r in range(1, 4):
             ccopy(i, r).wait_recv()
         total = ob[i, 0].astype(F32)
@@ -366,10 +386,6 @@
 
         @pl.when(it == 0)
         def _():
-            project_sum()
-
-        @pl.when(it == 1)
-        def _():
             project_send()
 
         @pl.when((it >= 2) & (it < 2 + PIECES))
@@ -385,6 +401,8 @@
         def _():
             down_copy.wait()
             wwaits[4].wait_recv()
+            for cp in wcopies + sycopies + sgcopies:
+                cp.wait_send()
 
         run(stage4, LAG4)
         run(stage5, LAG5)
@@ -408,26 +426,8 @@
         rest = (back - high.astype(F32)).astype(BF16)
         mixed_ref[:, q * 256:(q + 1) * 256] = (dot_t(pick_s[q], high) + dot_t(pick_s[q], rest)).astype(BF16)
 
-    for cp in wcopies + sycopies + sgcopies + [lcc]:
-        cp.wait_send()
-
-    def drain(i, carry):
-        for kind in range(10):
-            ycopy(kind, i).wait_send()
-        for r in range(1, 4):
-            ccopy(i, r).wait_send()
-            xcopy(i, r).wait_send()
-            sxcopy(i, r).wait_send()
-
-        @pl.when(i > 0)
-        def _():
-            zcopy(i).wait_send()
-            zscopy(i).wait_send()
-            rcopy_back(i).wait_send()
-
-        return carry
-
-    lax.fori_loop(0, PIECES, drain, 0)
+    lcc.wait_send()
+    returned(PIECES - 1)
 
 
 def moe(ids, route, tokens, cotangent, gate, up, down, projector):

time: 99.2 us -> 98.7 us (level); the launches traced: 99.1 us -> 97 us
  Pallas kernels: 98.5 us -> 96.3 us
    pallas_call x1, Pallas kernels: 94.1 us -> 91.9 us  [moe(): pl.pallas_call(moe_kernel, out_shape=(jax.ShapeDtypeStruct((64, 768), BF1...]
where the time goes in v4:
time: 98.7 us; the launch traced here: 97 us
  Pallas kernels  96.3 us (98%)
    pallas_call x1, Pallas kernels, moe(): pl.pallas_call(moe_kernel, out_shape=(jax.ShapeDtypeStruct((64, 768), BF1...  91.9 us
    pallas_call x1, Pallas kernels, update_step(): pl.pallas_call(update_kernel, out_shape=(jax.ShapeDtypeStruct((512, 768),...  4.42 us

profile of v4, /device:TPU:8, one launch (start us, length us, event | category | flops | bytes accessed | tf_op | source)
XLA Modules:
  0.0 97.0 jit_solution(17185428349623558519)
XLA Ops:
  0.6 91.9 %moe.1 = (bf16[64,768]{1,0:T(8,128)(2,1)}, bf16[512,512]{1,0:T(8,128)(2,1)}) custom-call(s32[2,64]{1,0:T(2,128)} %bitcast.3, f32[2,64]{1,0:T(2,128)} %bitcast.4, bf16[64,768]{1,0:T(8,128)(2,1)} %tok_hbm.1, bf16[64,768]{1,0:T(8,128)(2,1)} %cot_hbm.1, bf16[768,512]{1,0:T(8,128)(2,1)} %wg_hbm.1, bf16[768,512]{1,0:T(8,128)(2,1)} %wu_hbm.1, ...), custom_call_target="tpu_custom_call" | custom-call | flops 8000000000 | bytes 6000000 | tf_op jit(solution)/shard_map/moe/pallas_call | solution.py:453
  92.6 4.4 %update.1 = (f32[512,768]{1,0:T(8,128)}, f32[512,512]{1,0:T(8,128)}, f32[512,512]{1,0:T(8,128)}, bf16[64,768]{1,0:T(8,128)(2,1)}) custom-call(s32[1]{0:T(128)} %bitcast.expert_ref, bf16[512,512]{1,0:T(8,128)(2,1)} %get-tuple-element.10.low_ref, f32[512,512]{1,0:T(8,128)} %first_ref.1, f32[512,512]{1,0:T(8,128)} %second_ref.1, bf16[4,768,512]{2,1,0:T(8,128)(2,1)} %proj_ref.1, ...), custom_call_target="tpu_custom_call" | custom-call | flops 800000000 | bytes 7000000 | tf_op jit(solution)/shard_map/update/pallas_call | solution.py:493

commit v5 on v4

--- a/solution.py
+++ b/solution.py
@@ -377,26 +377,6 @@
         run(stage3, LAG3)
         run(stage2, LAG2)
         run(stage1, LAG1)
-        run(stage0, 0)
-
-        @pl.when(it + 1 < PIECES)
-        def _():
-            zcopy(it + 1).wait_recv()
-            spread(it + 1)
-
-        @pl.when(it == 0)
-        def _():
-            project_send()
-
-        @pl.when((it >= 2) & (it < 2 + PIECES))
-        def _():
-            @pl.when(it > 2)
-            def _():
-                zscopy(it - 2).wait_recv()
-
-            for r in (2, 1, 3):
-                sxcopy(it - 2, r).start()
-
         @pl.when(it == LAG4)
         def _():
             down_copy.wait()
@@ -406,6 +386,26 @@
 
         run(stage4, LAG4)
         run(stage5, LAG5)
+        run(stage0, 0)
+
+        @pl.when(it + 1 < PIECES)
+        def _():
+            zcopy(it + 1).wait_recv()
+            spread(it + 1)
+
+        @pl.when(it == 0)
+        def _():
+            project_send()
+
+        @pl.when((it >= 2) & (it < 2 + PIECES))
+        def _():
+            @pl.when(it > 2)
+            def _():
+                zscopy(it - 2).wait_recv()
+
+            for r in (2, 1, 3):
+                sxcopy(it - 2, r).start()
+
         return carry
 
     lax.fori_loop(0, PIECES + LAG4, step, 0)

time: 98.7 us -> 98.3 us (level)
  no operation moved by 1% of the time
where the time goes in v5:
time: 98.3 us; the launch traced here: 96.9 us
  Pallas kernels  96.3 us (98%)
    pallas_call x1, Pallas kernels, moe(): pl.pallas_call(moe_kernel, out_shape=(jax.ShapeDtypeStruct((64, 768), BF1...  91.8 us
    pallas_call x1, Pallas kernels, update_step(): pl.pallas_call(update_kernel, out_shape=(jax.ShapeDtypeStruct((512, 768),...  4.42 us

profile of v5, /device:TPU:8, one launch (start us, length us, event | category | flops | bytes accessed | tf_op | source)
XLA Modules:
  0.0 96.9 jit_solution(5366920213711890774)
XLA Ops:
  0.6 91.8 %moe.1 = (bf16[64,768]{1,0:T(8,128)(2,1)}, bf16[512,512]{1,0:T(8,128)(2,1)}) custom-call(s32[2,64]{1,0:T(2,128)} %bitcast.3, f32[2,64]{1,0:T(2,128)} %bitcast.4, bf16[64,768]{1,0:T(8,128)(2,1)} %tok_hbm.1, bf16[64,768]{1,0:T(8,128)(2,1)} %cot_hbm.1, bf16[768,512]{1,0:T(8,128)(2,1)} %wg_hbm.1, bf16[768,512]{1,0:T(8,128)(2,1)} %wu_hbm.1, ...), custom_call_target="tpu_custom_call" | custom-call | flops 8000000000 | bytes 6000000 | tf_op jit(solution)/shard_map/moe/pallas_call | solution.py:453
  92.5 4.4 %update.1 = (f32[512,768]{1,0:T(8,128)}, f32[512,512]{1,0:T(8,128)}, f32[512,512]{1,0:T(8,128)}, bf16[64,768]{1,0:T(8,128)(2,1)}) custom-call(s32[1]{0:T(128)} %bitcast.expert_ref, bf16[512,512]{1,0:T(8,128)(2,1)} %get-tuple-element.10.low_ref, f32[512,512]{1,0:T(8,128)} %first_ref.1, f32[512,512]{1,0:T(8,128)} %second_ref.1, bf16[4,768,512]{2,1,0:T(8,128)(2,1)} %proj_ref.1, ...), custom_call_target="tpu_custom_call" | custom-call | flops 800000000 | bytes 7000000 | tf_op jit(solution)/shard_map/update/pallas_call | solution.py:493
